TPU v7x, 32 devices: a whole 2x2x4 slice. The times are simulated.
32 devices in a mesh: row: 8 (over y, x, core), head: 4 (over z).
Axes of the slice: x: 2, y: 2, z: 4, core: 2. Of those that a mesh axis runs over, the one named last changes fastest.
Arguments:
- activations: bfloat16 [16384, 768], P('row', 'head'), may hold values from -6 to 6
- segment_ids: int32 [16, 1024], P('row'), may hold values from 0 to 31, never falling along the last dimension, each value on 1 to 512 neighbouring positions
- block_lists: int32 [16, 12, 16, 4], P('row', 'head'), may hold values from -1 to 15, as said below
- feature_proj: bfloat16 [64, 256], replicated, may hold values from -5 to 5
- input_norm_gain: float32 [768], replicated, may hold values from 0.1 to 1.9
- input_norm_bias: float32 [768], replicated, may hold values from -1.5 to 1.5
- qkv_weight: bfloat16 [768, 2304], P(None, 'head'), may hold values from -0.21875 to 0.21875
- out_weight: bfloat16 [768, 768], P('head'), may hold values from -0.875 to 0.875
- middle_norm_gain: float32 [768], replicated, may hold values from 0.2 to 6
- middle_norm_bias: float32 [768], replicated, may hold values from -1.5 to 1.5
- up_weight: bfloat16 [768, 3072], P(None, 'head'), may hold values from -0.21875 to 0.21875
- down_weight: bfloat16 [3072, 768], P('head'), may hold values from -0.109375 to 0.109375
- out_grad: bfloat16 [16384, 768], P('row', 'head'), may hold values from -6 to 6
Outputs:
- block_out: bfloat16 [16384, 768], P('row', 'head')
- input_grad: float32 [16384, 768], P('row', 'head')
- norm_gain_grad: float32 [768], P('head')
- norm_shift_grad: float32 [768], P('head')
- qkv_weight_grad: float32 [768, 2304], P(None, 'head')
- out_weight_grad: float32 [768, 768], P('head')
- middle_norm_gain_gradient: float32 [768], P('head')
- middle_norm_bias_gradient: float32 [768], P('head')
- up_weight_grad: float32 [768, 3072], P(None, 'head')
- down_weight_grad: float32 [3072, 768], P('head')
Inputs may be any that keep to these rules, and one draw needn't show every extreme that they name: `segment_ids`: never falling along a sequence; equal numbers in one sequence mark one document, which may be as long as 512 tokens. `block_lists`: each list holds its used entries first, at least one, and -1 in the slots after them; used entries are key blocks of the same sequence and may repeat.
All inputs are finite; a program needn't handle non-finite values.
Results may differ from a plain program's by a relative error of at most 0.018.
Values may be sent and summed in bfloat16 or wider, within the bound.
No kernel may reach another device: no remote copies, remote signals or barrier semaphores. Data moves between devices by JAX's collectives and lax.ppermute only.
A program may use at most 192 MiB of HBM per device.

v0:
```python
from functools import partial

import math
import jax, jax.numpy as jnp
from jax import lax
from jax.experimental import pallas as pl
from jax.experimental.pallas import tpu as pltpu

BLK = 64
CHUNK = 1024
LOG2E = 1.4426950408889634

def dot(a, b, dims):
    return lax.dot_general(a, b, (dims, ((), ())), preferred_element_type=jnp.float32)

def meets(seg_ref, r0, tq, c0, tk):
    return (seg_ref[0, r0] <= seg_ref[0, c0 + tk - 1]) & (seg_ref[0, c0] <= seg_ref[0, r0 + tq - 1])

def fwd_kernel(at_ref, seg_s, own_ref, oth_ref, segc_ref, segr_ref, hit_ref, proj_ref, *rest, tq, tk, dh, part):
    (out_ref, rinv_ref, *early, done_ref, vext, qf_ref, kf_ref, qkv_ref, w_ref, wo_ref, sems) = rest[-(15 if part == 0 else 17):]
    sums, early = early[:-5], early[-5:]
    done_ref[0] = 0
    cut = w_ref.shape[1]
    slots = [at_ref[0] ^ d for d in range(4)]
    copies = [
        pltpu.make_async_copy(piece.at[part, pl.ds(0, cut), :], w_ref.at[slots[d]], sems.at[0, d])
        for d, piece in enumerate(rest[:4])
    ] + [
        pltpu.make_async_copy(piece.at[part, pl.ds(cut, wo_ref.shape[1]), :], wo_ref.at[slots[d]], sems.at[1, d])
        for d, piece in enumerate(rest[:4])
    ]
    for copy in copies:
        copy.start()
    for copy in copies:
        copy.wait()
    leaving = [
        pltpu.make_async_copy(src, dst, sems.at[2 + i // 4, i % 4])
        for i, (src, dst) in enumerate(zip((qf_ref, kf_ref, qkv_ref, w_ref, wo_ref), early))
    ]
    leaving[3].start()
    leaving[4].start()
    weights = w_ref[...].reshape(qkv_ref.shape[1], own_ref.shape[1])
    for side, n_ref in enumerate((own_ref, oth_ref)):
        half = n_ref.shape[0]
        qkv_ref[side * half:(side + 1) * half, :] = dot(n_ref[...], weights, ((1,), (1,))).astype(jnp.bfloat16)
    length = qkv_ref.shape[0]
    feats = proj_ref.shape[1]
    quarter = dh ** (-0.25)
    nh = qkv_ref.shape[1] // (3 * dh)
    for h in range(nh):
        base = h * 3 * dh
        for j, f_ref in ((0, qf_ref), (1, kf_ref)):
            for r0 in range(0, length, CHUNK):
                rows = slice(r0, r0 + CHUNK)
                t = qkv_ref[rows, base + j * dh: base + (j + 1) * dh]
                lin = dot(t, proj_ref[...], ((1,), (0,)))
                tw = t.astype(jnp.float32)
                sq = jnp.sum(tw * tw, axis=1, keepdims=True) * (0.5 * quarter * quarter * LOG2E) + 0.5 * math.log2(feats)
                f_ref[h, rows, :] = jnp.exp2(lin * (quarter * LOG2E) - sq).astype(jnp.bfloat16)
        v = qkv_ref[:, base + 2 * dh: base + 3 * dh]
        lane = lax.broadcasted_iota(jnp.int32, (length, dh), 1)
        vext[h, :, :] = jnp.concatenate([v, (lane < 1).astype(jnp.bfloat16)], axis=1)

    for copy in leaving[:3]:
        copy.start()

    def q_body(i, _):
        r0 = pl.multiple_of(i * tq, tq)
        qs = [qkv_ref[pl.ds(r0, tq), h * 3 * dh: h * 3 * dh + dh] for h in range(nh)]
        qfs = [qf_ref[h, pl.ds(r0, tq), :] for h in range(nh)]
        segq = segc_ref[pl.ds(r0, tq), :]
        def k_body(j, acc):
            c0 = pl.multiple_of(j * tk, tk)
            same = segq == segr_ref[:, pl.ds(c0, tk)]
            new = []
            for h in range(nh):
                k = qkv_ref[pl.ds(c0, tk), h * 3 * dh + dh: h * 3 * dh + 2 * dh]
                s = dot(qs[h], k, ((1,), (1,)))
                e = jnp.exp2(s * (LOG2E * dh ** -0.5))
                a = dot(qfs[h], kf_ref[h, pl.ds(c0, tk), :], ((1,), (1,)))
                parts = []
                for b in range(tq // BLK):
                    hit = hit_ref[h, pl.ds(i * (tq // BLK) + b, 1), pl.ds(c0, tk)] > 0.5
                    rs = slice(b * BLK, (b + 1) * BLK)
                    parts.append(jnp.where(jnp.broadcast_to(hit, (BLK, tk)), e[rs], a[rs]))
                comb = jnp.where(same, jnp.concatenate(parts, axis=0), 0.0).astype(jnp.bfloat16)
                new.append(acc[h] + dot(comb, vext[h, pl.ds(c0, tk), :], ((1,), (0,))))
            return tuple(new)
        def k_step(j, acc):
            return lax.cond(meets(seg_s, r0, tq, pl.multiple_of(j * tk, tk), tk), lambda a: k_body(j, a), lambda a: a, acc)
        acc = lax.fori_loop(0, length // tk, k_step, tuple(jnp.zeros((tq, 2 * dh), jnp.float32) for _ in range(nh)))
        for h in range(nh):
            rinv = 1.0 / acc[h][:, dh:dh + 1]
            out_ref[pl.ds(r0, tq), h * dh:(h + 1) * dh] = (acc[h][:, :dh] * rinv).astype(jnp.bfloat16)
            rinv_ref[pl.ds(r0, tq), h:h + 1] = rinv
        return 0
    lax.fori_loop(0, length // tq, q_body, 0)

    if part:
        other, w_other = rest[4], rest[5]
        w_first = w_other[...].reshape(out_ref.shape[1], own_ref.shape[1])
        w_out = wo_ref[...].reshape(out_ref.shape[1], own_ref.shape[1])
        add_parts(
            lambda rows: dot(other[rows, :], w_first, ((1,), (0,))) + dot(out_ref[rows, :], w_out, ((1,), (0,))),
            None, sums, length, False,
        )
    for copy in leaving:
        copy.wait()


def add_parts(product, before, sums, length, first):
    half = length // 2
    for side in range(2):
        rows = slice(side * half, (side + 1) * half)
        part = product(rows)
        if first:
            sums[0][rows, :] = part
        else:
            total = part if before is None else part + before[rows, :]
            sums[side][...] = total.astype(sums[side].dtype)


def sum_shapes(length, width, first):
    whole = lambda n, dtype: jax.ShapeDtypeStruct((n, width), dtype)
    return [whole(length, jnp.float32)] if first else [whole(length // 2, jnp.float32), whole(length // 2, jnp.bfloat16)]


def attn_fwd(at, n_own, n_oth, pieces, part, seg, hit, proj, before=(), ahead=(), *, tq=512, tk=512):
    length, width = 2 * n_own.shape[0], n_own.shape[1]
    dh, feats = proj.shape
    heads = hit.shape[0]
    cols = 3 * heads * dh
    seg2 = seg.reshape(1, length)
    bf16 = jnp.bfloat16
    smem = pl.BlockSpec(memory_space=pltpu.SMEM)
    vmem = pl.BlockSpec(memory_space=pltpu.VMEM)
    anywhere = pl.BlockSpec(memory_space=pltpu.HBM)
    early = [
        ((heads, length, feats), bf16), ((heads, length, feats), bf16), ((length, cols), bf16),
        ((4, cols // 4, width), bf16), ((4, heads * dh // 4, width), bf16),
    ]
    sums = sum_shapes(length, width, False) if part else []
    return pl.pallas_call(
        partial(fwd_kernel, tq=tq, tk=tk, dh=dh, part=part),
        in_specs=[smem] * 2 + [vmem] * 6 + [anywhere] * 4 + [vmem] * len(before) + [anywhere] * len(ahead),
        out_specs=[vmem] * (2 + len(sums)) + [anywhere] * 5 + [smem],
        out_shape=[jax.ShapeDtypeStruct((length, heads * dh), bf16), jax.ShapeDtypeStruct((length, 8), jnp.float32)]
        + sums
        + [jax.ShapeDtypeStruct(*v) for v in early]
        + [jax.ShapeDtypeStruct((1,), jnp.int32)],
        scratch_shapes=[pltpu.VMEM((heads, length, 2 * dh), bf16)]
        + [pltpu.VMEM(*v) for v in early]
        + [pltpu.SemaphoreType.DMA((4, 4))],
        compiler_params=pltpu.CompilerParams(vmem_limit_bytes=48 * 1024 * 1024),
        cost_estimate=pl.CostEstimate(flops=27 * 10**9, bytes_accessed=10**7, transcendentals=10**6),
        name="attn_fwd",
    )(at, seg2, n_own, n_oth, seg.reshape(length, 1), seg2, hit, proj, *pieces, *before, *ahead)


def bwd_kernel(at_ref, seg_s, qkv_ref, segc_ref, segr_ref, hit_ref, proj_ref, pext_ref, qf_ref, kf_ref, rinv_ref, o_ref,
               d_own, d_oth, w_out, *rest, tq, tk, dh, first):
    n_late = 3 if first else 5
    (*outs, done_ref, dqkv_s, do_ref, grad_s, vext, doext, dq, dk, dv, dqf, dkf, late_sem) = rest[-(14 if first else 18) - n_late:-n_late]
    late = rest[-n_late:]
    n_own, n_oth, w_ref = late[:3]
    arriving = [pltpu.make_async_copy(src, dst, late_sem.at[i]) for i, (src, dst) in enumerate(zip(rest, late))]
    for copy in arriving:
        copy.start()
    dqkv_ref = outs[1] if first else dqkv_s
    done_ref[0] = 0
    length = qkv_ref.shape[0]
    half = length // 2
    quarter = dh ** (-0.25)
    nh = qkv_ref.shape[1] // (3 * dh)
    for side, d_ref in enumerate((d_own, d_oth)):
        do_ref[side * half:(side + 1) * half, :] = dot(d_ref[...], w_out[...], ((1,), (1,))).astype(jnp.bfloat16)
    lane = lax.broadcasted_iota(jnp.int32, (length, dh), 1)
    for h in range(nh):
        base = h * 3 * dh
        v = qkv_ref[:, base + 2 * dh: base + 3 * dh]
        vext[h, :, :] = jnp.concatenate([v, (lane < 2).astype(jnp.bfloat16)], axis=1)
        d_o = do_ref[:, h * dh:(h + 1) * dh].astype(jnp.float32)
        o = o_ref[:, h * dh:(h + 1) * dh].astype(jnp.float32)
        rinv = rinv_ref[:, h:h + 1]
        delta = -jnp.sum(d_o * o, axis=1, keepdims=True) * rinv
        high = delta.astype(jnp.bfloat16).astype(jnp.float32)
        low = delta - high
        tail = jnp.where(lane == 0, high, jnp.where(lane == 1, low, 0.0))
        doext[h, :, :] = jnp.concatenate([d_o * rinv, tail], axis=1).astype(jnp.bfloat16)
    dq[...] = jnp.zeros_like(dq)
    dk[...] = jnp.zeros_like(dk)
    dv[...] = jnp.zeros_like(dv)
    dqf[...] = jnp.zeros_like(dqf)
    dkf[...] = jnp.zeros_like(dkf)

    def q_body(i, _):
        r0 = pl.multiple_of(i * tq, tq)
        rows = pl.ds(r0, tq)
        segq = segc_ref[rows, :]
        def k_body(j, _):
            c0 = pl.multiple_of(j * tk, tk)
            cols = pl.ds(c0, tk)
            same = segq == segr_ref[:, cols]
            for h in range(nh):
                base = h * 3 * dh
                q = qkv_ref[rows, base: base + dh]
                k = qkv_ref[cols, base + dh: base + 2 * dh]
                qf = qf_ref[h, rows, :]
                kf = kf_ref[h, cols, :]
                s = dot(q, k, ((1,), (1,)))
                e = jnp.exp2(s * (LOG2E * dh ** -0.5))
                a = dot(qf, kf, ((1,), (1,)))
                dc = dot(doext[h, rows, :], vext[h, cols, :], ((1,), (1,)))
                dc = jnp.where(same, dc, 0.0)
                combs, dss, das = [], [], []
                for b in range(tq // BLK):
                    hit = hit_ref[h, pl.ds(i * (tq // BLK) + b, 1), cols] > 0.5
                    hit = jnp.broadcast_to(hit, (BLK, tk))
                    rs = slice(b * BLK, (b + 1) * BLK)
                    combs.append(jnp.where(hit, e[rs], a[rs]))
                    dss.append(jnp.where(hit, dc[rs] * e[rs], 0.0))
                    das.append(jnp.where(hit, 0.0, dc[rs]))
                comb = jnp.where(same, jnp.concatenate(combs, axis=0), 0.0).astype(jnp.bfloat16)
                ds = jnp.concatenate(dss, axis=0).astype(jnp.bfloat16)
                da = jnp.concatenate(das, axis=0).astype(jnp.bfloat16)
                dq[h, rows, :] += dot(ds, k, ((1,), (0,)))
                dqf[h, rows, :] += dot(da, kf, ((1,), (0,)))
                dk[h, cols, :] += dot(ds, q, ((0,), (0,)))
                dkf[h, cols, :] += dot(da, qf, ((0,), (0,)))
                dv[h, cols, :] += dot(comb, doext[h, rows, :dh], ((0,), (0,)))
            return 0
        def k_step(j, _):
            @pl.when(meets(seg_s, r0, tq, pl.multiple_of(j * tk, tk), tk))
            def _():
                k_body(j, 0)
            return 0
        lax.fori_loop(0, length // tk, k_step, 0)
        return 0
    lax.fori_loop(0, length // tq, q_body, 0)

    for h in range(nh):
        base = h * 3 * dh
        for j, dt, dfeat, f_ref in ((0, dq, dqf, qf_ref), (1, dk, dkf, kf_ref)):
            for r0 in range(0, length, CHUNK):
                rows = slice(r0, r0 + CHUNK)
                dpre = (dfeat[h, rows, :] * f_ref[h, rows, :].astype(jnp.float32)).astype(jnp.bfloat16)
                thr = dot(dpre, pext_ref[...], ((1,), (0,)))
                t = qkv_ref[rows, base + j * dh: base + (j + 1) * dh].astype(jnp.float32)
                g = dt[h, rows, :] * dh ** -0.5 + quarter * thr[:, :dh] - (quarter * quarter) * t * thr[:, dh:dh + 1]
                dqkv_ref[rows, base + j * dh: base + (j + 1) * dh] = g.astype(jnp.bfloat16)
        dqkv_ref[:, base + 2 * dh: base + 3 * dh] = dv[h].astype(jnp.bfloat16)

    for copy in arriving:
        copy.wait()
    if not first:
        dqkv_first, w_first = late[3:]
        weights = w_ref[...].reshape(qkv_ref.shape[1], n_own.shape[1])
        weights_first = w_first[...].reshape(qkv_ref.shape[1], n_own.shape[1])
        add_parts(
            lambda rows: dot(dqkv_first[rows, :], weights_first, ((1,), (0,))) + dot(dqkv_ref[rows, :], weights, ((1,), (0,))),
            None, outs[4:], length, False,
        )

    tn = ((0,), (0,))
    cut = w_ref.shape[1]
    grad = dot(dqkv_ref[:half, :], n_own[...], tn) + dot(dqkv_ref[half:, :], n_oth[...], tn)
    grad_s[:, :cut, :] = grad.astype(jnp.bfloat16).reshape(4, cut, n_own.shape[1])
    out = dot(o_ref[:half, :], d_own[...], tn) + dot(o_ref[half:, :], d_oth[...], tn)
    grad_s[:, cut:, :] = out.astype(jnp.bfloat16).reshape(4, o_ref.shape[1] // 4, n_own.shape[1])
    if first:
        outs[0][...] = grad_s[...]
    else:
        for d in range(4):
            outs[d][...] = grad_s[at_ref[0] ^ d]


def attn_bwd(at, qkv, seg, hit, proj, qf, kf, rinv, o, d_own, d_oth, w_out, late, ahead=(), *, tq=512, tk=256):
    length = qkv.shape[0]
    dh, feats = proj.shape
    width = d_own.shape[1]
    heads = qkv.shape[1] // (3 * dh)
    seg2 = seg.reshape(1, length)
    pext = jnp.concatenate([proj.T, jnp.ones((feats, 1), proj.dtype), jnp.zeros((feats, dh - 1), proj.dtype)], axis=1)
    f32, bf16 = jnp.float32, jnp.bfloat16
    smem = pl.BlockSpec(memory_space=pltpu.SMEM)
    vmem = pl.BlockSpec(memory_space=pltpu.VMEM)
    anywhere = pl.BlockSpec(memory_space=pltpu.HBM)
    first = len(late) == 3
    piece = jax.ShapeDtypeStruct(((qkv.shape[1] + o.shape[1]) // 4, width), bf16)
    if first:
        outs = [jax.ShapeDtypeStruct((4,) + piece.shape, bf16), jax.ShapeDtypeStruct(qkv.shape, bf16)]
    else:
        outs = [piece] * 4 + sum_shapes(length, width, False)
    return pl.pallas_call(
        partial(bwd_kernel, tq=tq, tk=tk, dh=dh, first=first),
        in_specs=[smem] * 2 + [vmem] * 13 + [anywhere] * (len(late) + len(ahead)),
        out_specs=[vmem] * len(outs) + [smem],
        out_shape=outs + [jax.ShapeDtypeStruct((1,), jnp.int32)],
        scratch_shapes=[
            pltpu.VMEM((16, 128) if first else qkv.shape, bf16),
            pltpu.VMEM(o.shape, bf16),
            pltpu.VMEM((4,) + piece.shape, bf16),
            pltpu.VMEM((heads, length, 2 * dh), bf16),
            pltpu.VMEM((heads, length, 2 * dh), bf16),
            pltpu.VMEM((heads, length, dh), f32),
            pltpu.VMEM((heads, length, dh), f32),
            pltpu.VMEM((heads, length, dh), f32),
            pltpu.VMEM((heads, length, feats), f32),
            pltpu.VMEM((heads, length, feats), f32),
            pltpu.SemaphoreType.DMA((5,)),
        ]
        + [pltpu.VMEM(v.shape, v.dtype) for v in late],
        compiler_params=pltpu.CompilerParams(vmem_limit_bytes=56 * 1024 * 1024),
        cost_estimate=pl.CostEstimate(flops=42 * 10**9, bytes_accessed=2 * 10**7, transcendentals=10**6),
        name="attn_bwd",
    )(at, seg2, qkv, seg.reshape(length, 1), seg2, hit, proj, pext, qf, kf, rinv, o, d_own, d_oth, w_out, *late, *ahead)


def hit_lanes(lists, length):
    nb = lists.shape[1]
    ids = lax.broadcasted_iota(jnp.int32, (1, 1, length), 2) // BLK
    out = lists[:, :, 0:1] == ids
    for s in range(1, lists.shape[2]):
        out = out | (lists[:, :, s:s + 1] == ids)
    return out.astype(jnp.float32)

from jax.sharding import PartitionSpec as P


def gelu_pair(u):
    mag = jnp.abs(u)
    t = 1.0 / (1.0 + (0.3275911 * 0.7071067811865476) * mag)
    bell = jnp.exp2(u * u * (-0.5 * LOG2E))
    poly = t * (0.127414796 + t * (-0.142248368 + t * (0.7107068705 + t * (-0.7265760135 + t * 0.5307027145))))
    tail = poly * bell
    cdf = jnp.where(u >= 0.0, 1.0 - tail, tail)
    return u * cdf, cdf + u * bell * 0.3989422804014327


def mlp_kernel(n_own, n_oth, dy_own, dy_oth, w_ref, *rest, first):
    act_ref, dpre_ref, *sums = rest[-(3 if first else 4):]
    half, width = n_own.shape
    piece = w_ref.shape[1] // 2
    hid = act_ref.shape[1]
    up = w_ref[:, :piece, :].reshape(width, hid)
    down = w_ref[:, piece:, :].reshape(hid, width)
    for side, (n_ref, dy_ref) in enumerate(((n_own, dy_own), (n_oth, dy_oth))):
        rs = slice(side * half, (side + 1) * half)
        pre = dot(n_ref[...], up, ((1,), (0,)))
        d_act = dot(dy_ref[...], down, ((1,), (1,)))
        act, slope = gelu_pair(pre)
        d_pre = (d_act * slope).astype(jnp.bfloat16)
        act_ref[rs, :] = act.astype(jnp.bfloat16)
        dpre_ref[rs, :] = d_pre
        part = dot(d_pre, up, ((1,), (1,)))
        if first:
            sums[0][rs, :] = part
        else:
            sums[side][...] = (part + rest[0][rs, :]).astype(sums[side].dtype)


def mlp_first(n2, dy, pack, before=None, ahead=()):
    tokens, width = 2 * n2[0].shape[0], n2[0].shape[1]
    hid = pack.shape[0] * pack.shape[1] // 2
    bf16, f32 = jnp.bfloat16, jnp.float32
    first = before is None
    vmem = pl.BlockSpec(memory_space=pltpu.VMEM)
    return pl.pallas_call(
        partial(mlp_kernel, first=first),
        in_specs=[vmem] * (5 if first else 6) + [pl.BlockSpec(memory_space=pltpu.HBM)] * len(ahead),
        out_specs=[vmem] * (3 if first else 4),
        out_shape=[jax.ShapeDtypeStruct((tokens, hid), bf16)] * 2 + sum_shapes(tokens, width, first),
        compiler_params=pltpu.CompilerParams(vmem_limit_bytes=48 * 1024 * 1024),
        cost_estimate=pl.CostEstimate(flops=2 * 10**9, bytes_accessed=2 * 10**6, transcendentals=10**6),
        name="mlp_first",
    )(*n2, *dy, pack, *(() if first else (before,)), *ahead)


def mlp_grad_kernel(n_own, n_oth, dy_own, dy_oth, act_ref, dpre_ref, *rest):
    grad_ref = rest[-1]
    half, width = n_own.shape
    piece = grad_ref.shape[3] // 2
    hid = act_ref.shape[1]
    tn = ((0,), (0,))
    for j in range(width // (4 * piece)):
        cut = slice(4 * j * piece, 4 * (j + 1) * piece)
        up_g = dot(n_own[:, cut], dpre_ref[:half, :], tn) + dot(n_oth[:, cut], dpre_ref[half:, :], tn)
        grad_ref[2 * j:2 * j + 2, :, 0, :piece, :] = up_g.astype(jnp.bfloat16).reshape(2, 2, piece, hid)
        down_g = dot(act_ref[:half, cut], dy_own[...], tn) + dot(act_ref[half:, cut], dy_oth[...], tn)
        grad_ref[2 * j:2 * j + 2, :, 0, piece:, :] = down_g.astype(jnp.bfloat16).reshape(2, 2, piece, width)


def mlp_second(n2, dy, acted, d_pre, rows, grads=None):
    width = n2[0].shape[1]
    whole = lambda shape: pl.BlockSpec(shape, lambda i: (0,) * len(shape))
    args = [*n2, *dy, acted, d_pre]
    first = grads is None
    shape = (4, 2, 2, rows, width)
    return pl.pallas_call(
        mlp_grad_kernel,
        grid=(1,),
        in_specs=[whole(v.shape) for v in args] + [pl.BlockSpec(memory_space=pltpu.HBM)] * (not first),
        out_specs=pl.BlockSpec((4, 2, 1) + shape[3:], lambda i: (0, 0, 0 if first else 1, 0, 0)),
        out_shape=jax.ShapeDtypeStruct(shape, jnp.bfloat16),
        input_output_aliases={} if first else {len(args): 0},
        compiler_params=pltpu.CompilerParams(vmem_limit_bytes=48 * 1024 * 1024),
        cost_estimate=pl.CostEstimate(flops=2 * 10**9, bytes_accessed=2 * 10**6, transcendentals=0),
        name="mlp_second",
    )(*args, *([] if first else [grads]))


def mlp_out_kernel(act_a, act_b, w_a, w_b, *rest):
    half, width = rest[-1].shape
    piece = w_a.shape[1] // 2
    downs = [w[:, piece:, :].reshape(-1, width) for w in (w_a, w_b)]
    for side, out_ref in enumerate(rest[-2:]):
        rows = slice(side * half, (side + 1) * half)
        total = dot(act_a[rows, :], downs[0], ((1,), (0,))) + dot(act_b[rows, :], downs[1], ((1,), (0,)))
        out_ref[...] = total.astype(out_ref.dtype)


def call(kernel, name, args, outs, ahead=(), smem=(), scratch=(), passed=()):
    vmem = pl.BlockSpec(memory_space=pltpu.VMEM)
    anywhere = pl.BlockSpec(memory_space=pltpu.HBM)
    n_in = len(smem) + len(args)
    return pl.pallas_call(
        kernel,
        in_specs=[pl.BlockSpec(memory_space=pltpu.SMEM)] * len(smem)
        + [vmem] * len(args)
        + [anywhere] * (len(passed) + len(ahead)),
        out_specs=[vmem] * len(outs) + [anywhere] * len(passed),
        out_shape=list(outs) + [jax.ShapeDtypeStruct(v.shape, v.dtype) for v in passed],
        input_output_aliases={n_in + i: len(outs) + i for i in range(len(passed))},
        scratch_shapes=list(scratch),
        compiler_params=pltpu.CompilerParams(vmem_limit_bytes=48 * 1024 * 1024),
        cost_estimate=pl.CostEstimate(flops=10**9, bytes_accessed=4 * 10**6, transcendentals=0),
        name=name,
    )(*smem, *args, *passed, *ahead)


norm_eps = 1e-05


def norm_rows(values):
    center = values - jnp.mean(values, axis=1, keepdims=True)
    scale = lax.rsqrt(jnp.mean(center * center, axis=1, keepdims=True) + norm_eps)
    return center * scale, scale


def norm_back(grad, xhat, scale, gain):
    dx = grad * gain
    return scale * (
        dx - jnp.mean(dx, axis=1, keepdims=True) - xhat * jnp.mean(dx * xhat, axis=1, keepdims=True)
    )


ROWS = 128


def enter_kernel(dealt_ref, gain_ref, bias_ref, *rest):
    x_ref, n_ref = rest[-2:]
    width = x_ref.shape[1]
    for i in range(x_ref.shape[0] // ROWS):
        rows = slice(i * ROWS, (i + 1) * ROWS)
        x = dealt_ref[:, :, rows].reshape(width, ROWS).astype(jnp.float32).T
        x_ref[rows, :] = x.astype(jnp.bfloat16)
        n_ref[rows, :] = (norm_rows(x)[0] * gain_ref[...] + bias_ref[...]).astype(jnp.bfloat16)


def turn_kernel(z_ref, d0, d1, d2, d3, *rest):
    out_ref, turned = rest[-4], rest[-1]
    for d, part in enumerate((d0, d1, d2, d3)):
        turned[z_ref[0] ^ d] = part[...]
    for i in range(out_ref.shape[0] // ROWS):
        rows = slice(i * ROWS, (i + 1) * ROWS)
        out_ref[rows, :] = turned[:, :, rows].reshape(out_ref.shape[1], ROWS).astype(jnp.float32).T.astype(jnp.bfloat16)


def pick_kernel(which_ref, own_ref, got_ref, *rest):
    out_ref = rest[-1]
    rows = pl.ds(pl.multiple_of(which_ref[1] * out_ref.shape[0], 16), out_ref.shape[0])

    @pl.when(which_ref[0] == 1)
    def _():
        out_ref[...] = own_ref[rows, :]

    @pl.when(which_ref[0] == 0)
    def _():
        out_ref[...] = got_ref[rows, :]


def middle_kernel(x_ref, near_ref, got_ref, gain_ref, bias_ref, *rest):
    resid_ref, n_ref = rest[-2:]
    for i in range(x_ref.shape[0] // ROWS):
        rows = slice(i * ROWS, (i + 1) * ROWS)
        resid = x_ref[rows, :].astype(jnp.float32) + near_ref[rows, :] + got_ref[rows, :].astype(jnp.float32)
        resid_ref[rows, :] = resid
        xhat = norm_rows(resid.astype(jnp.bfloat16).astype(jnp.float32))[0]
        n_ref[rows, :] = (xhat * gain_ref[...] + bias_ref[...]).astype(jnp.bfloat16)


def middle_back_kernel(own_ref, got_ref, resid_ref, dy_ref, gain_ref, *rest):
    d_ref, low_ref, vec_ref = rest[-3:]
    total = None
    for i in range(own_ref.shape[0] // ROWS):
        rows = slice(i * ROWS, (i + 1) * ROWS)
        grad = own_ref[rows, :] + got_ref[rows, :].astype(jnp.float32)
        xhat, scale = norm_rows(resid_ref[rows, :].astype(jnp.bfloat16).astype(jnp.float32))
        sums = [jnp.sum(grad * xhat, axis=0, keepdims=True), jnp.sum(grad, axis=0, keepdims=True)]
        total = sums if total is None else [a + b for a, b in zip(total, sums)]
        d = dy_ref[rows, :].astype(jnp.float32) + norm_back(grad, xhat, scale, gain_ref[...])
        d_ref[rows, :] = d
        low_ref[rows, :] = d.astype(jnp.bfloat16)
    vec_ref[0:1, :] = total[0]
    vec_ref[1:2, :] = total[1]


def block_kernel(resid_ref, own_ref, got_ref, *rest):
    out_ref = rest[-1]
    parts, quarter, _ = out_ref.shape
    for i in range(own_ref.shape[0] // ROWS):
        rows = slice(i * ROWS, (i + 1) * ROWS)
        out = resid_ref[rows, :] + own_ref[rows, :] + got_ref[rows, :].astype(jnp.float32)
        out_ref[:, :, rows] = out.T.astype(jnp.bfloat16).reshape(parts, quarter, ROWS)


def leave_kernel(near_ref, got_ref, x_ref, d_ref, gain_ref, vec_ref, *rest):
    out_ref = rest[-1]
    parts, quarter = out_ref.shape[0], near_ref.shape[1] // out_ref.shape[0]
    total = None
    for i in range(near_ref.shape[0] // ROWS):
        rows = slice(i * ROWS, (i + 1) * ROWS)
        grad = near_ref[rows, :] + got_ref[rows, :].astype(jnp.float32)
        xhat, scale = norm_rows(x_ref[rows, :].astype(jnp.float32))
        sums = [jnp.sum(grad * xhat, axis=0, keepdims=True), jnp.sum(grad, axis=0, keepdims=True)]
        total = sums if total is None else [a + b for a, b in zip(total, sums)]
        out = d_ref[rows, :] + norm_back(grad, xhat, scale, gain_ref[...])
        out_ref[:, :quarter, rows] = out.T.astype(jnp.bfloat16).reshape(parts, quarter, ROWS)
    vec = jnp.concatenate(total + [vec_ref[0:1, :], vec_ref[1:2, :]], axis=0)
    high = vec.astype(jnp.bfloat16).astype(jnp.float32)
    both = jnp.concatenate([high, vec - high], axis=0)
    tail = out_ref.shape[1] - quarter
    for k in range(parts):
        mine = both[:, k * quarter:(k + 1) * quarter]
        mine = jnp.concatenate([mine, jnp.zeros((8, out_ref.shape[2] - quarter), jnp.float32)], axis=1)
        mine = jnp.concatenate([mine, jnp.zeros((tail - 8, out_ref.shape[2]), jnp.float32)], axis=0)
        out_ref[k, quarter:, :] = mine.astype(jnp.bfloat16)


def sum_kernel(a, b, c, d, *rest, out_at):
    total = a[...].astype(jnp.float32) + b[...].astype(jnp.float32) + c[...].astype(jnp.float32) + d[...].astype(jnp.float32)
    rest[out_at][...] = total.astype(jnp.bfloat16)


def split_kernel(both_ref, a_ref, b_ref):
    cut = a_ref.shape[1]
    a_ref[...] = both_ref[:, :cut, :].astype(jnp.float32)
    b_ref[...] = both_ref[:, cut:, :].astype(jnp.float32)


def sum_slices_kernel(a, *rest):
    rest[-2][...] = jnp.sum(a[...].astype(jnp.float32), axis=0).astype(jnp.bfloat16)


def sum_four(pieces, name, ahead=(), passed=()):
    out = [jax.ShapeDtypeStruct(pieces[0].shape, jnp.bfloat16)]
    at = len(passed) + len(ahead)
    return call(partial(sum_kernel, out_at=at), name, pieces, out, ahead=ahead, passed=passed)


def own_group(i):
    return (i & 3) // 2 == (i >> 2) & 1


def far_group(i):
    return not own_group(i)


def shards(
    activations, segment_ids, block_lists, feature_proj, input_norm_gain, input_norm_bias, qkv_weight,
    out_weight, middle_norm_gain, middle_norm_bias, up_weight, down_weight, out_grad,
):
    rows_n, heads_n = lax.axis_size("row"), lax.axis_size("head")
    total = rows_n * heads_n
    r, z = lax.axis_index("row"), lax.axis_index("head")
    c, p = r % 2, (r // 2) % 4
    groups = rows_n // 8
    pairs = [[2 * i, 2 * i + 1] for i in range(rows_n // 2)]
    planes = [[8 * g + i for i in range(8)] for g in range(groups)]
    quads = [[8 * g + 2 * i + k for i in range(4)] for g in range(groups) for k in range(2)]
    width = input_norm_gain.shape[0]
    quarter = width // heads_n
    seq_count, length = segment_ids.shape
    half = length // 2
    lists_here = block_lists.shape[1]
    bf16, f32 = jnp.bfloat16, jnp.float32
    local = (z // 2) == c
    par = z % 2

    def move(v, mask, only=None):
        moves = [(i, i ^ mask) for i in range(total) if only is None or only(i)]
        return lax.ppermute(v, ("row", "head"), moves)

    def later(i, dep):
        one = lax.slice(dep, (0,) * dep.ndim, (1,) * dep.ndim).reshape(())
        return i + (one != one).astype(jnp.int32)

    def deal_z(v):
        return lax.all_to_all(v, "head", 0, 0, tiled=True)

    def tied(v, dep):
        one = lax.slice(dep, (0,) * dep.ndim, (1,) * dep.ndim).reshape(())
        return v + (one != one).astype(v.dtype)

    def deal(v, side, order):
        v = v.T

        def token_half(k):
            return jnp.stack([lax.dynamic_slice_in_dim(v, s * length + k * half, half, 1) for s in range(seq_count)])

        keep, got = token_half(side), move(token_half(1 - side), 4)
        return jnp.concatenate([jnp.where(order == 0, keep, got), jnp.where(order == 0, got, keep)], 0)

    def collect(v):
        v = v.reshape(2, seq_count, quarter, half)
        keep = lax.dynamic_index_in_dim(v, c, 0, keepdims=False)
        got = move(lax.dynamic_index_in_dim(v, 1 - c, 0, keepdims=False), 4)
        low, high = jnp.where(c == 0, keep, got), jnp.where(c == 0, got, keep)
        return jnp.concatenate([w[s] for s in range(seq_count) for w in (low, high)], 1).T

    def fetch_z(mine):
        return [mine] + [move(mine, d, own_group) for d in (1, 2, 3)]

    def choose(got, here):
        return jnp.stack([jnp.where(here, got[0], got[2]), jnp.where(here, got[1], got[3])])

    def fetch_plane(both):
        return [both] + [move(both, 8 * d) for d in (1, 2, 3)]

    def give_z(same, other, ahead, before_slice):
        parts = (same, move(other, 1, own_group), move(same, 2, far_group), move(other, 3, far_group))
        (fin,) = sum_four(parts, "sum_z", ahead=(ahead,))
        if groups > 1:
            fin = lax.psum(fin.astype(f32), "row", axis_index_groups=[[8 * g + i for g in range(groups)] for i in range(8)])
            fin = fin.astype(bf16)
        return call(
            pick_kernel, "pick", (fin, move(fin, 4)), (jax.ShapeDtypeStruct((fin.shape[0] // 2, width), bf16),),
            smem=(jnp.stack([local.astype(jnp.int32), c]),), ahead=(before_slice,),
        )[0]

    def gather_plane(v):
        return lax.all_gather(v, "row", axis=0, axis_index_groups=planes)

    cut = lambda w, n, at: lax.dynamic_slice_in_dim(w, at * n, n, 0)

    aux = jnp.concatenate([block_lists.reshape(seq_count, -1), segment_ids], 1).astype(bf16)
    aux_got = move(aux, 4)
    aux = jnp.where(c == 0, jnp.concatenate([aux, aux_got], 0), jnp.concatenate([aux_got, aux], 0))
    n_list = aux.shape[1] - length
    seg = lax.dynamic_index_in_dim(aux[:, n_list:], z, 0, keepdims=False).astype(jnp.int32)

    n_qkv, n_out = qkv_weight.shape[1] // 4, out_weight.shape[0] // 4
    extra = 16
    rider = aux[:, :n_list].reshape(-1)
    rider = jnp.pad(rider, (0, extra * width - rider.shape[0])).reshape(extra, width)
    mine = [cut(qkv_weight.T, n_qkv, p), cut(out_weight, n_out, p), rider]
    both = choose(fetch_z(jnp.concatenate(mine, 0)), local)
    lists = both[:, n_qkv + n_out:].reshape(2, -1)[:, :4 * n_list].reshape(2, 4, n_list).astype(jnp.int32)
    lists = lax.dynamic_index_in_dim(lists, z, 1, keepdims=False).reshape((2, lists_here) + block_lists.shape[2:])
    pieces = fetch_plane(both[:, :n_qkv + n_out])
    at = jnp.full((1,), p, jnp.int32)

    four = deal(activations, c, later(c, both))
    gain1, bias1, gain2, bias2 = (
        v.reshape(1, width) for v in (input_norm_gain, input_norm_bias, middle_norm_gain, middle_norm_bias)
    )
    shape_of = jax.ShapeDtypeStruct
    half_low, half_wide = shape_of((half, width), bf16), shape_of((half, width), f32)
    dy_four = deal(out_grad, c, c)
    x_half, n1_half = call(enter_kernel, "enter", (deal_z(four), gain1, bias1), (half_low, half_low), ahead=(dy_four,))

    n_up, n_hid = width // 8, down_weight.shape[0] // 8
    q8 = later(r % 8, both)
    mine = jnp.concatenate([cut(up_weight, n_up, q8), cut(down_weight, n_hid, q8)], 0)
    all_z = lax.all_gather(mine, "head", axis=0).reshape((1, 2, 2) + mine.shape)
    send = [jnp.broadcast_to(all_z[:, :, i], (4, 2) + mine.shape).reshape((8,) + mine.shape) for i in range(2)]
    packs = [lax.all_to_all(v, "row", 0, 0, axis_index_groups=planes, tiled=True) for v in send]

    shift = c * half
    seg = lax.dynamic_slice_in_dim(jnp.concatenate([seg, seg]), shift, length, 0)
    hits = []
    for own in lists:
        own = lax.dynamic_slice_in_dim(jnp.concatenate([own, own], 1), shift // BLK, length // BLK, 1)
        hit = hit_lanes(own, length)
        hits.append(lax.dynamic_slice_in_dim(jnp.concatenate([hit, hit], 2), shift, length, 2))

    n1 = (n1_half, move(n1_half, 4))
    att = [attn_fwd(at, *n1, pieces, 0, seg, hits[0], feature_proj)]
    z_late = z + att[0][-1][0]
    dy_parts = [lax.dynamic_index_in_dim(dy_four, z_late ^ d, 0, keepdims=False) for d in range(heads_n)]
    dy_got = [move(v, d) if d else v for d, v in enumerate(dy_parts)]
    att.append(attn_fwd(at, *n1, pieces, 1, seg, hits[1], feature_proj, (att[0][0], att[0][6]), (*send, *dy_parts)))
    heads_out = [v[0] for v in att]
    rinv = [v[1] for v in att]
    feat_q, feat_k, qkv, wq, outw = zip(*(v[-6:-1] for v in att))
    outw = [v.reshape(-1, width) for v in outw]
    dy_half, near, away = call(
        turn_kernel, "turn", dy_got, (half_low,), smem=(z.reshape(1),), passed=att[1][2:4], ahead=(packs[0],),
        scratch=(pltpu.VMEM((heads_n, quarter, half), bf16),),
    )
    resid, n2_half = call(
        middle_kernel, "middle", (x_half, near, move(away, 4), gain2, bias2), (half_wide, half_low),
    )
    n2 = (n2_half, move(n2_half, 4))
    dy = (dy_half, move(dy_half, 4))
    acted, d_pre, dn = mlp_first(n2, dy, packs[0])
    grads = mlp_second(n2, dy, acted, d_pre, packs[0].shape[1])
    acted_a = acted
    acted, d_pre, dn_own, dn_oth = mlp_first(n2, dy, packs[1], dn, (grads,))
    grads = mlp_second(n2, dy, acted, d_pre, packs[1].shape[1], grads)
    mo_own, mo_oth = call(
        mlp_out_kernel, "mlp_out", (acted_a, acted, *packs), (half_wide, half_low), ahead=(grads,)
    )
    d_resid, d_half, vec2 = call(
        middle_back_kernel, "middle_back", (dn_own, move(dn_oth, 4), resid, dy_half, gain2),
        (half_wide, half_low, shape_of((2, width), f32)),
    )
    (block_send,) = call(
        block_kernel, "block", (resid, mo_own, move(mo_oth, 4)), (shape_of((heads_n, quarter, half), bf16),)
    )
    block_got = deal_z(block_send)
    block_out = collect(block_got)
    d_branch = (d_half, move(d_half, 4))
    grads = lax.psum_scatter(
        grads.reshape(-1, width), "row", scatter_dimension=0, axis_index_groups=quads, tiled=True
    ).reshape(2, 2, -1, width)
    def attn_back(i, late, ahead):
        return attn_bwd(
            at, qkv[i], seg, hits[i], feature_proj, feat_q[i], feat_k[i], rinv[i], heads_out[i], *d_branch, outw[i],
            (*n1, wq[i], *late), ahead,
        )

    back = [attn_back(0, (), (mo_oth,))]
    c_late = later(c + back[0][2][0], block_got)
    keep = lax.dynamic_index_in_dim(grads, c_late, 0, keepdims=False)
    got = move(lax.dynamic_index_in_dim(grads, 1 - c_late, 0, keepdims=False), 4)
    four = jnp.concatenate([jnp.where(c == 0, keep, got), jnp.where(c == 0, got, keep)], 0)
    four_flat = four.reshape(-1, width)
    mlp_slice = mlp_grads = lax.psum_scatter(four_flat, "head", scatter_dimension=0, tiled=True)
    if groups > 1:
        mlp_grads = lax.psum(mlp_grads, "row", axis_index_groups=[[8 * g + i for g in range(groups)] for i in range(8)])

    back.append(attn_back(1, (back[0][1], wq[0]), (block_got, four_flat)))

    def across(pieces):
        return [pieces[0]] + [move(pieces[d], 8 * d) for d in (1, 2, 3)]

    first = lax.all_to_all(back[0][0], "row", 0, 0, axis_index_groups=quads, tiled=True)
    first, *passed = call(
        sum_slices_kernel, "sum_first", (first,), (shape_of(first.shape[1:], bf16),), passed=(mlp_grads,), ahead=(back[1][0],)
    )
    (mlp_grads,) = passed
    pieces, (near, away) = back[1][:4], back[1][4:6]
    mlp_grads = gather_plane(mlp_grads)
    up_grad = mlp_grads[:, :n_up].reshape(width, -1).astype(f32)
    down_grad = mlp_grads[:, n_up:].reshape(-1, width).astype(f32)
    (send,) = call(
        leave_kernel, "leave", (near, move(away, 4), x_half, d_resid, gain1, vec2),
        (shape_of((heads_n, quarter + 16, half), bf16),), ahead=(first,),
    )
    (second,) = sum_four(across(pieces), "sum_second", ahead=(send,))
    got = deal_z(send)
    qkv_slice = give_z(first, second, got, mlp_grads)
    input_grad = collect(got[:, :quarter]).astype(f32)
    vec = jnp.sum(got[:, quarter:quarter + 8, :quarter].astype(f32), 0)
    got = gather_plane(qkv_slice)
    vec = tied(vec[:4] + vec[4:], qkv_slice)
    for mask in (4, 8, 16):
        vec = vec + move(vec, mask)
    if groups > 1:
        vec = lax.psum(vec, "row", axis_index_groups=[[8 * g + i for g in range(groups)] for i in range(8)])
    qkv_grad, out_w_grad = call(
        split_kernel, "split", (got.reshape(4, n_qkv + n_out, width),),
        (shape_of((4, n_qkv, width), f32), shape_of((4, n_out, width), f32)),
    )
    qkv_grad = qkv_grad.reshape(-1, width).T
    out_w_grad = out_w_grad.reshape(-1, width)
    return (
        block_out, input_grad, vec[0], vec[1], qkv_grad, out_w_grad, vec[2], vec[3], up_grad, down_grad,
    )


def solution(mesh):
    return jax.shard_map(
        shards,
        mesh=mesh,
        in_specs=(
            P("row", "head"), P("row", None), P("row", "head", None, None), P(), P(), P(), P(None, "head"),
            P("head", None), P(), P(), P(None, "head"), P("head", None), P("row", "head"),
        ),
        out_specs=(
            P("row", "head"), P("row", "head"), P("head"), P("head"), P(None, "head"), P("head", None),
            P("head"), P("head"), P(None, "head"), P("head", None),
        ),
        check_vma=False,
    )
```

profile of v0, /device:TPU:0, one launch (start us, length us, event | category | flops | bytes accessed | tf_op | source)
XLA Modules:
  0.0 373.6 jit_solution(17359883980729929909)
XLA Ops:
  7.3 1.7 dynamic-slice_bitcast_fusion.7
  12.0 5.8 %collective-permute-start.1 = (bf16[208,768]{1,0:T(8,128)(2,1)}, bf16[208,768]{1,0:T(8,128)(2,1)S(1)}, u32[]{:S(2)}, u32[]{:S(2)}) collective-permute-start(bf16[208,768]{1,0:T(8,128)(2,1)} %pad_maximum_fusion.8), channel_id=1, source_target_pairs={{0,2},{1,3},{6,4},{7,5},{8,10},{9,11},{14,12},{15,13},{16,18},{17,... | collective-permute-start | bytes 958472 | tf_op jit(solution)/shard_map/ppermute | solution.py:602
  18.7 3.5 collective-permute-start.5
  28.4 3.7 %collective-permute-done.5 = bf16[208,768]{1,0:T(8,128)(2,1)S(1)} collective-permute-done((bf16[208,768]{1,0:T(8,128)(2,1)}, bf16[208,768]{1,0:T(8,128)(2,1)S(1)}, u32[]{:S(2)}, u32[]{:S(2)}) %collective-permute-start.5) | collective-permute-done | bytes 319520 | tf_op jit(solution)/shard_map/ppermute | solution.py:602
  34.2 5.3 %all-to-all-start = ((bf16[4,192,512]{2,1,0:T(8,128)(2,1)}), bf16[4,192,512]{2,1,0:T(8,128)(2,1)S(1)}, u32[]{:S(2)}, u32[]{:S(2)}) async-start(bf16[4,192,512]{2,1,0:T(8,128)(2,1)} %pad_maximum_fusion.2), calls=%async_computation | async-start | bytes 1572864 | tf_op jit(solution)/shard_map/all_to_all | solution.py:609
  39.6 1.6 collective-permute-start.7
  41.1 1.5 collective-permute-start.8
  45.6 30.7 %all-to-all-done.dealt_ref = bf16[4,192,512]{2,1,0:T(8,128)(2,1)S(1)} async-done(((bf16[4,192,512]{2,1,0:T(8,128)(2,1)}), bf16[4,192,512]{2,1,0:T(8,128)(2,1)S(1)}, u32[]{:S(2)}, u32[]{:S(2)}) %all-to-all-start) | async-done | bytes 786464 | tf_op jit(solution)/shard_map/all_to_all | solution.py:609
  76.3 1.7 enter.1
  78.6 2.2 slice_bitcast_fusion
  80.8 1.6 broadcast_in_dim.19
  82.4 4.7 %all-to-all-start.1 = ((bf16[8,192,768]{2,1,0:T(8,128)(2,1)}), bf16[8,192,768]{2,1,0:T(8,128)(2,1)}, u32[]{:S(2)}, u32[]{:S(2)}) async-start(bf16[8,192,768]{2,1,0:T(8,128)(2,1)} %bitcast.168), calls=%async_computation.1 | async-start | bytes 4718592 | tf_op jit(solution)/shard_map/all_to_all | solution.py:687
  87.1 17.7 %attn_fwd.2 = (bf16[1024,192]{1,0:T(8,128)(2,1)S(1)}, f32[1024,8]{1,0:T(8,128)S(1)}, bf16[3,1024,256]{2,1,0:T(8,128)(2,1)}, bf16[3,1024,256]{2,1,0:T(8,128)(2,1)...) custom-call(s32[1]{0:T(128)} %bitcast.20.at_ref, ...), custom_call_target="tpu_custom_call" | custom-call | flops 27000000512 | bytes 10000000 | tf_op jit(solution)/shard_map/attn_fwd/pallas_call | solution.py:143
  107.9 2.3 fusion.7
  110.2 2.0 collective-permute-start.11
  112.3 2.3 collective-permute-start.12
  114.6 1.6 broadcast_in_dim.21
  116.2 19.7 %attn_fwd.3 = (bf16[1024,192]{1,0:T(8,128)(2,1)S(1)}, f32[1024,8]{1,0:T(8,128)S(1)}, f32[512,768]{1,0:T(8,128)}, bf16[512,768]{1,0:T(8,128)(2,1)}, bf16[3,1024,2...) custom-call(s32[1]{0:T(128)} %bitcast.20.at_ref, ...), custom_call_target="tpu_custom_call" | custom-call | flops 27000000512 | bytes 10000000 | tf_op jit(solution)/shard_map/attn_fwd/pallas_call | solution.py:143
  138.2 4.5 %all-to-all-start.2 = ((bf16[8,192,768]{2,1,0:T(8,128)(2,1)}), bf16[8,192,768]{2,1,0:T(8,128)(2,1)}, u32[]{:S(2)}, u32[]{:S(2)}) async-start(bf16[8,192,768]{2,1,0:T(8,128)(2,1)} %bitcast.171), calls=%async_computation.2 | async-start | bytes 4718592 | tf_op jit(solution)/shard_map/all_to_all | solution.py:687
  148.6 1.7 collective-permute-done.13.got_ref
  154.0 2.0 collective-permute-done.14.n_oth
  155.9 8.3 %mlp_first.2 = (bf16[1024,768]{1,0:T(8,128)(2,1)S(1)}, bf16[1024,768]{1,0:T(8,128)(2,1)}, f32[1024,768]{1,0:T(8,128)}) custom-call(bf16[512,768]{1,0:T(8,128)(2,1)S(1)} %get-tuple-element.69.n_own, bf16[512,768]{1,0:T(8,128)(2,1)S(1)} %collective-permute-done.14.n_oth, bf16[512,768]{1,0:T(8,128)(2,1)S(1)} %get-tuple-element.70.dy_own.dy_ref, ...), custom_call_target="tpu_custom_call" | custom-call | flops 2000000000 | bytes 2000000 | tf_op jit(solution)/shard_map/mlp_first/pallas_call | solution.py:368
  164.2 5.4 %mlp_second.2.rest_1_.rest_0_ = bf16[4,2,2,192,768]{4,3,2,1,0:T(8,128)(2,1)} custom-call(bf16[512,768]{1,0:T(8,128)(2,1)S(1)} %get-tuple-element.69.n_own, bf16[512,768]{1,0:T(8,128)(2,1)S(1)} %collective-permute-done.14.n_oth, bf16[512,768]{1,0:T(8,128)(2,1)S(1)} %get-tuple-element.70.dy_own.dy_ref, bf16[512,768]{1,0:T(8,128)(2,1)S(1)} %collective-permute-done.15.dy_oth, ...), custom_call_target="tpu_custom_call" | custom-call | flops 2000000000 | bytes 2000000 | tf_op jit(solution)/shard_map/mlp_second/pallas_call | solution.py:399
  172.2 9.4 %mlp_first.3 = (bf16[1024,768]{1,0:T(8,128)(2,1)S(1)}, bf16[1024,768]{1,0:T(8,128)(2,1)}, f32[512,768]{1,0:T(8,128)}, bf16[512,768]{1,0:T(8,128)(2,1)}) custom-call(bf16[512,768]{1,0:T(8,128)(2,1)S(1)} %get-tuple-element.69.n_own, bf16[512,768]{1,0:T(8,128)(2,1)S(1)} %collective-permute-done.14.n_oth, bf16[512,768]{1,0:T(8,128)(2,1)S(1)} %get-tuple-element.70.dy_own.dy_ref, ...), custom_call_target="tpu_custom_call" | custom-call | flops 2000000000 | bytes 2000000 | tf_op jit(solution)/shard_map/mlp_first/pallas_call | solution.py:368
  181.6 6.1 %mlp_second.3.rest_0_ = bf16[4,2,2,192,768]{4,3,2,1,0:T(8,128)(2,1)} custom-call(bf16[512,768]{1,0:T(8,128)(2,1)S(1)} %get-tuple-element.69.n_own, bf16[512,768]{1,0:T(8,128)(2,1)S(1)} %collective-permute-done.14.n_oth, bf16[512,768]{1,0:T(8,128)(2,1)S(1)} %get-tuple-element.70.dy_own.dy_ref, ...), custom_call_target="tpu_custom_call", output_to_operand_aliasing={{}: (6, {})} | custom-call | flops 2000000000 | bytes 2000000 | tf_op jit(solution)/shard_map/mlp_second/pallas_call | solution.py:399
  190.5 6.5 %mlp_out.1 = (f32[512,768]{1,0:T(8,128)S(1)}, bf16[512,768]{1,0:T(8,128)(2,1)}) custom-call(bf16[1024,768]{1,0:T(8,128)(2,1)S(1)} %copy-done.5, bf16[1024,768]{1,0:T(8,128)(2,1)S(1)} %copy-done.7, bf16[8,192,768]{2,1,0:T(8,128)(2,1)} %all-to-all-done.1.rest_2_.w_ref.w_a, bf16[8,192,768]{2,1,0:T(8,128)(2,1)} %all-to-all-done.2.w_ref.w_b, ...), custom_call_target="tpu_custom_call" | custom-call | flops 1000000000 | bytes 4000000 | tf_op jit(solution)/shard_map/mlp_out/pallas_call | solution.py:426
  198.2 3.9 %middle_back.1 = (f32[512,768]{1,0:T(8,128)S(1)}, bf16[512,768]{1,0:T(8,128)(2,1)}, f32[2,768]{1,0:T(2,128)S(1)}) custom-call(f32[512,768]{1,0:T(8,128)S(1)} %copy-done.18, bf16[512,768]{1,0:T(8,128)(2,1)S(1)} %collective-permute-done.18.got_ref, f32[512,768]{1,0:T(8,128)} %copy-done.2, bf16[512,768]{1,0:T(8,128)(2,1)S(1)} %get-tuple-element.70.dy_own.dy_ref, ...), custom_call_target="tpu_custom_call" | custom-call | flops 1000000000 | bytes 4000000 | tf_op jit(solution)/shard_map/middle_back/pallas_call | solution.py:426
  204.6 1.5 copy-done.17
  207.4 3.7 all-to-all-start.3
  211.9 26.4 %attn_bwd.2 = (bf16[4,192,768]{2,1,0:T(8,128)(2,1)}, bf16[1024,576]{1,0:T(8,128)(2,1)}, s32[1]{0:T(128)}) custom-call(s32[1]{0:T(128)} %bitcast.20.at_ref, s32[1,1024]{1,0:T(1,128)} %bitcast.160, bf16[1024,576]{1,0:T(8,128)(2,1)} %get-tuple-element.88.qkv_ref, s32[1024,1]{1,0:T(8,128)} %copy.43.segc_ref, s32[1,1024]{1,0:T(1,128)} %bitcast.161, ...), custom_call_target="tpu_custom_call" | custom-call | flops 41999998976 | bytes 20000000 | tf_op jit(solution)/shard_map/attn_bwd/pallas_call | solution.py:294
  240.9 2.1 reduce-scatter.3.cloned.1.call-done
  244.2 3.5 all-to-all-start.4
  250.4 29.4 %attn_bwd.3 = (bf16[192,768]{1,0:T(8,128)(2,1)}, bf16[192,768]{1,0:T(8,128)(2,1)}, bf16[192,768]{1,0:T(8,128)(2,1)}, bf16[192,768]{1,0:T(8,128)(2,1)}, f32[512,7...) custom-call(s32[1]{0:T(128)} %bitcast.20.at_ref, s32[1,1024]{1,0:T(1,128)} %bitcast.162, ...), custom_call_target="tpu_custom_call" | custom-call | flops 41999998976 | bytes 20000000 | tf_op jit(solution)/shard_map/attn_bwd/pallas_call | solution.py:294
  286.3 2.6 collective-permute-done.21.got_ref
  290.0 3.6 leave.1.rest_0_
  293.6 3.9 %all-to-all-start.5 = ((bf16[4,208,512]{2,1,0:T(8,128)(2,1)}), bf16[4,208,512]{2,1,0:T(8,128)(2,1)S(1)}, u32[]{:S(2)}, u32[]{:S(2)}) async-start(bf16[4,208,512]{2,1,0:T(8,128)(2,1)} %leave.1.rest_0_), calls=%async_computation.7 | async-start | bytes 1703936 | tf_op jit(solution)/shard_map/all_to_all | solution.py:609
  299.5 1.5 collective-permute-start.23
  305.8 6.0 %collective-permute-done.23.b = bf16[192,768]{1,0:T(8,128)(2,1)S(1)} collective-permute-done((bf16[192,768]{1,0:T(8,128)(2,1)}, bf16[192,768]{1,0:T(8,128)(2,1)S(1)}, u32[]{:S(2)}, u32[]{:S(2)}) %collective-permute-start.23) | collective-permute-done | bytes 294944 | tf_op jit(solution)/shard_map/ppermute | solution.py:602
  311.8 5.9 %collective-permute-done.24.c = bf16[192,768]{1,0:T(8,128)(2,1)S(1)} collective-permute-done((bf16[192,768]{1,0:T(8,128)(2,1)}, bf16[192,768]{1,0:T(8,128)(2,1)S(1)}, u32[]{:S(2)}, u32[]{:S(2)}) %collective-permute-start.24) | collective-permute-done | bytes 294944 | tf_op jit(solution)/shard_map/ppermute | solution.py:602
  317.6 4.8 %collective-permute-done.25.d = bf16[192,768]{1,0:T(8,128)(2,1)S(1)} collective-permute-done((bf16[192,768]{1,0:T(8,128)(2,1)S(1)}, bf16[192,768]{1,0:T(8,128)(2,1)S(1)}, u32[]{:S(2)}, u32[]{:S(2)}) %collective-permute-start.25) | collective-permute-done | bytes 294944 | tf_op jit(solution)/shard_map/ppermute | solution.py:602
  322.5 3.9 %collective-permute-start.26 = (bf16[192,768]{1,0:T(8,128)(2,1)S(1)}, bf16[192,768]{1,0:T(8,128)(2,1)S(1)}, u32[]{:S(2)}, u32[]{:S(2)}) collective-permute-start(bf16[192,768]{1,0:T(8,128)(2,1)S(1)} %sum_second.1), channel_id=1, source_target_pairs={{0,1},{1,0},{6,7},{7,6},{8,9},{9,8},{14,15},{15,14},{16,17},{17,16... | collective-permute-start | bytes 884744 | tf_op jit(solution)/shard_map/ppermute | solution.py:602
  327.9 1.7 collective-permute-start.22
  329.6 2.1 maximum_bitcast_fusion
  331.7 5.3 %collective-permute-done.28.d = bf16[192,768]{1,0:T(8,128)(2,1)S(1)} collective-permute-done((bf16[192,768]{1,0:T(8,128)(2,1)S(1)}, bf16[192,768]{1,0:T(8,128)(2,1)S(1)}, u32[]{:S(2)}, u32[]{:S(2)}) %collective-permute-start.28) | collective-permute-done | bytes 294944 | tf_op jit(solution)/shard_map/ppermute | solution.py:602
  338.8 1.7 copy-done.8
  348.2 1.7 bitcast_convert_fusion.1
  350.9 1.7 bitcast_convert_fusion
  354.6 9.3 %all-gather.11.cloned.1.call-done = bf16[768,768]{1,0:T(8,128)(2,1)} async-done(((bf16[96,768]{1,0:T(8,128)(2,1)}), bf16[768,768]{1,0:T(8,128)(2,1)}) %all-gather.11.cloned.1.call-update) | async-done | bytes 1179664 | tf_op jit(solution)/shard_map/all_gather | solution.py:652
  (280 shorter events, 73.8 us)
Async XLA Ops:
  7.2 71.4 %all-gather.7.cloned.1.call-start = ((), (), s32[]{:S(2)}) async-start(), calls=%async_computation.10 | async-start | bytes 1474560 | tf_op jit(solution)/shard_map/all_gather | solution.py:685
  9.0 23.1 %collective-permute-start.2 = (bf16[2,192,512]{2,1,0:T(8,128)(2,1)S(1)}, bf16[2,192,512]{2,1,0:T(8,128)(2,1)}, u32[]{:S(2)}, u32[]{:S(2)}) collective-permute-start(bf16[2,192,512]{2,1,0:T(8,128)(2,1)S(1)} %pad_maximum_fusion.5), channel_id=1, source_target_pairs={{0,4},{1,5},{2,6},{3,7},{4,0},{5,1},{6,2},{7,3},{8,12},{9,13},{10,... | collective-permute-start | bytes 1179656 | tf_op jit(solution)/shard_map/ppermute | solution.py:602
  9.9 1.2 collective-permute-start
  12.0 12.7 %collective-permute-start.1 = (bf16[208,768]{1,0:T(8,128)(2,1)}, bf16[208,768]{1,0:T(8,128)(2,1)S(1)}, u32[]{:S(2)}, u32[]{:S(2)}) collective-permute-start(bf16[208,768]{1,0:T(8,128)(2,1)} %pad_maximum_fusion.8), channel_id=1, source_target_pairs={{0,2},{1,3},{6,4},{7,5},{8,10},{9,11},{14,12},{15,13},{16,18},{17,... | collective-permute-start | bytes 958472 | tf_op jit(solution)/shard_map/ppermute | solution.py:602
  18.6 25.2 %collective-permute-start.3 = (bf16[2,192,512]{2,1,0:T(8,128)(2,1)}, bf16[2,192,512]{2,1,0:T(8,128)(2,1)}, u32[]{:S(2)}, u32[]{:S(2)}) collective-permute-start(bf16[2,192,512]{2,1,0:T(8,128)(2,1)} %pad_maximum_fusion.7), channel_id=1, source_target_pairs={{0,4},{1,5},{2,6},{3,7},{4,0},{5,1},{6,2},{7,3},{8,12},{9,13},{10,... | collective-permute-start | bytes 1179656 | tf_op jit(solution)/shard_map/ppermute | solution.py:602
  18.6 57.7 %copy-start.34 = (f32[1,768]{1,0:T(1,128)}, f32[1,768]{1,0:T(1,128)S(1)}, u32[]{:S(2)}) copy-start(f32[1,768]{1,0:T(1,128)S(1)} %reshape.171.gain_ref) | copy-start | bytes 9220
  18.7 13.4 %collective-permute-start.5 = (bf16[208,768]{1,0:T(8,128)(2,1)}, bf16[208,768]{1,0:T(8,128)(2,1)S(1)}, u32[]{:S(2)}, u32[]{:S(2)}) collective-permute-start(bf16[208,768]{1,0:T(8,128)(2,1)} %pad_maximum_fusion.8), channel_id=1, source_target_pairs={{0,1},{1,0},{6,7},{7,6},{8,9},{9,8},{14,15},{15,14},{16,17},{17,16... | collective-permute-start | bytes 958472 | tf_op jit(solution)/shard_map/ppermute | solution.py:602
  22.2 9.9 %collective-permute-start.6 = (bf16[208,768]{1,0:T(8,128)(2,1)}, bf16[208,768]{1,0:T(8,128)(2,1)S(1)}, u32[]{:S(2)}, u32[]{:S(2)}) collective-permute-start(bf16[208,768]{1,0:T(8,128)(2,1)} %pad_maximum_fusion.8), channel_id=1, source_target_pairs={{0,3},{1,2},{6,5},{7,4},{8,11},{9,10},{14,13},{15,12},{16,19},{17,... | collective-permute-start | bytes 958472 | tf_op jit(solution)/shard_map/ppermute | solution.py:602
  23.7 92.5 %copy-start.33 = (s32[1024]{0:T(1024)}, s32[1024]{0:T(1024)S(1)}, u32[]{:S(2)}) copy-start(s32[1024]{0:T(1024)S(1)} %fusion.20) | copy-start | bytes 12292
  34.2 42.1 %all-to-all-start = ((bf16[4,192,512]{2,1,0:T(8,128)(2,1)}), bf16[4,192,512]{2,1,0:T(8,128)(2,1)S(1)}, u32[]{:S(2)}, u32[]{:S(2)}) async-start(bf16[4,192,512]{2,1,0:T(8,128)(2,1)} %pad_maximum_fusion.2), calls=%async_computation | async-start | bytes 1572864 | tf_op jit(solution)/shard_map/all_to_all | solution.py:609
  39.6 47.5 %collective-permute-start.7 = (bf16[2,192,768]{2,1,0:T(8,128)(2,1)S(1)}, bf16[2,192,768]{2,1,0:T(8,128)(2,1)}, u32[]{:S(2)}, u32[]{:S(2)}) collective-permute-start(bf16[2,192,768]{2,1,0:T(8,128)(2,1)S(1)} %pad_maximum_fusion.3.rest_0_), channel_id=1, source_target_pairs={{0,8},{1,9},{2,10},{3,11},{4,12},{5,13},{6,14},{7,15},{8,0},{9,1},... | collective-permute-start | bytes 1769480 | tf_op jit(solution)/shard_map/ppermute | solution.py:602
  41.1 45.9 %collective-permute-start.8 = (bf16[2,192,768]{2,1,0:T(8,128)(2,1)S(1)}, bf16[2,192,768]{2,1,0:T(8,128)(2,1)}, u32[]{:S(2)}, u32[]{:S(2)}) collective-permute-start(bf16[2,192,768]{2,1,0:T(8,128)(2,1)S(1)} %pad_maximum_fusion.3.rest_0_), channel_id=1, source_target_pairs={{0,16},{1,17},{2,18},{3,19},{4,20},{5,21},{6,22},{7,23},{8,24},{9,... | collective-permute-start | bytes 1769480 | tf_op jit(solution)/shard_map/ppermute | solution.py:602
  42.6 44.4 %collective-permute-start.9 = (bf16[2,192,768]{2,1,0:T(8,128)(2,1)S(1)}, bf16[2,192,768]{2,1,0:T(8,128)(2,1)}, u32[]{:S(2)}, u32[]{:S(2)}) collective-permute-start(bf16[2,192,768]{2,1,0:T(8,128)(2,1)S(1)} %pad_maximum_fusion.3.rest_0_), channel_id=1, source_target_pairs={{0,24},{1,25},{2,26},{3,27},{4,28},{5,29},{6,30},{7,31},{8,16},{9,... | collective-permute-start | bytes 1769480 | tf_op jit(solution)/shard_map/ppermute | solution.py:602
  78.0 72.3 %copy-start.21 = (bf16[512,768]{1,0:T(8,128)(2,1)}, bf16[512,768]{1,0:T(8,128)(2,1)S(1)}, u32[]{:S(2)}) copy-start(bf16[512,768]{1,0:T(8,128)(2,1)S(1)} %get-tuple-element.59.x_ref) | copy-start | bytes 2359300
  78.0 9.1 %collective-permute-start.4 = (bf16[512,768]{1,0:T(8,128)(2,1)}, bf16[512,768]{1,0:T(8,128)(2,1)S(1)}, u32[]{:S(2)}, u32[]{:S(2)}) collective-permute-start(bf16[512,768]{1,0:T(8,128)(2,1)} %get-tuple-element.60.own_ref.rest_0_), channel_id=1, source_target_pairs={{0,4},{1,5},{2,6},{3,7},{4,0},{5,1},{6,2},{7,3},{8,12},{9,13},{10,... | collective-permute-start | bytes 2359304 | tf_op jit(solution)/shard_map/ppermute | solution.py:602
  78.6 37.6 %copy-start.29 = (f32[3,16,1024]{2,1,0:T(8,128)}, f32[3,16,1024]{2,1,0:T(8,128)S(1)}, u32[]{:S(2)}) copy-start(f32[3,16,1024]{2,1,0:T(8,128)S(1)} %fusion.9.hit_ref) | copy-start | bytes 589828
  82.4 55.9 %all-to-all-start.1 = ((bf16[8,192,768]{2,1,0:T(8,128)(2,1)}), bf16[8,192,768]{2,1,0:T(8,128)(2,1)}, u32[]{:S(2)}, u32[]{:S(2)}) async-start(bf16[8,192,768]{2,1,0:T(8,128)(2,1)} %bitcast.168), calls=%async_computation.1 | async-start | bytes 4718592 | tf_op jit(solution)/shard_map/all_to_all | solution.py:687
  110.2 32.7 %collective-permute-start.10 = (bf16[192,512]{1,0:T(8,128)(2,1)}, bf16[192,512]{1,0:T(8,128)(2,1)S(1)}, u32[]{:S(2)}, u32[]{:S(2)}) collective-permute-start(bf16[192,512]{1,0:T(8,128)(2,1)} %get-tuple-element.122.rest_9_), channel_id=1, source_target_pairs={{0,1},{1,0},{2,3},{3,2},{4,5},{5,4},{6,7},{7,6},{8,9},{9,8},{10,11... | collective-permute-start | bytes 589832 | tf_op jit(solution)/shard_map/ppermute | solution.py:602
  110.2 32.6 %collective-permute-start.11 = (bf16[192,512]{1,0:T(8,128)(2,1)}, bf16[192,512]{1,0:T(8,128)(2,1)S(1)}, u32[]{:S(2)}, u32[]{:S(2)}) collective-permute-start(bf16[192,512]{1,0:T(8,128)(2,1)} %get-tuple-element.123.rest_10_), channel_id=1, source_target_pairs={{0,2},{1,3},{2,0},{3,1},{4,6},{5,7},{6,4},{7,5},{8,10},{9,11},{10,... | collective-permute-start | bytes 589832 | tf_op jit(solution)/shard_map/ppermute | solution.py:602
  112.3 31.3 %collective-permute-start.12 = (bf16[192,512]{1,0:T(8,128)(2,1)}, bf16[192,512]{1,0:T(8,128)(2,1)}, u32[]{:S(2)}, u32[]{:S(2)}) collective-permute-start(bf16[192,512]{1,0:T(8,128)(2,1)} %get-tuple-element.120.rest_11_), channel_id=1, source_target_pairs={{0,3},{1,2},{2,1},{3,0},{4,7},{5,6},{6,5},{7,4},{8,11},{9,10},{10,... | collective-permute-start | bytes 589832 | tf_op jit(solution)/shard_map/ppermute | solution.py:602
  138.2 34.0 %all-to-all-start.2 = ((bf16[8,192,768]{2,1,0:T(8,128)(2,1)}), bf16[8,192,768]{2,1,0:T(8,128)(2,1)}, u32[]{:S(2)}, u32[]{:S(2)}) async-start(bf16[8,192,768]{2,1,0:T(8,128)(2,1)} %bitcast.171), calls=%async_computation.2 | async-start | bytes 4718592 | tf_op jit(solution)/shard_map/all_to_all | solution.py:687
  142.8 100.3 %reduce-scatter.3.cloned.1.call-start = ((), (), s32[]{:S(2)}) async-start(), calls=%async_computation.8 | async-start | bytes 5898240 | tf_op jit(solution)/shard_map/reduce_scatter | solution.py:734
  148.0 2.3 collective-permute-start.13
  148.4 5.6 %collective-permute-start.15 = (bf16[512,768]{1,0:T(8,128)(2,1)S(1)}, bf16[512,768]{1,0:T(8,128)(2,1)S(1)}, u32[]{:S(2)}, u32[]{:S(2)}) collective-permute-start(bf16[512,768]{1,0:T(8,128)(2,1)S(1)} %get-tuple-element.70.dy_own.dy_ref), channel_id=1, source_target_pairs={{0,4},{1,5},{2,6},{3,7},{4,0},{5,1},{6,2},{7,3},{8,12},{9,13},{10,... | collective-permute-start | bytes 2359304 | tf_op jit(solution)/shard_map/ppermute | solution.py:602
  153.6 2.3 collective-permute-start.14
  187.7 10.4 %collective-permute-start.18 = (bf16[512,768]{1,0:T(8,128)(2,1)}, bf16[512,768]{1,0:T(8,128)(2,1)S(1)}, u32[]{:S(2)}, u32[]{:S(2)}) collective-permute-start(bf16[512,768]{1,0:T(8,128)(2,1)} %get-tuple-element.84), channel_id=1, source_target_pairs={{0,4},{1,5},{2,6},{3,7},{4,0},{5,1},{6,2},{7,3},{8,12},{9,13},{10,... | collective-permute-start | bytes 2359304 | tf_op jit(solution)/shard_map/ppermute | solution.py:602
  198.1 6.5 %collective-permute-start.16 = (bf16[512,768]{1,0:T(8,128)(2,1)}, bf16[512,768]{1,0:T(8,128)(2,1)S(1)}, u32[]{:S(2)}, u32[]{:S(2)}) collective-permute-start(bf16[512,768]{1,0:T(8,128)(2,1)} %get-tuple-element.77.rest_3_), channel_id=1, source_target_pairs={{0,4},{1,5},{2,6},{3,7},{4,0},{5,1},{6,2},{7,3},{8,12},{9,13},{10,... | collective-permute-start | bytes 2359304 | tf_op jit(solution)/shard_map/ppermute | solution.py:602
  203.2 7.8 %collective-permute-start.19 = (bf16[512,768]{1,0:T(8,128)(2,1)}, bf16[512,768]{1,0:T(8,128)(2,1)S(1)}, u32[]{:S(2)}, u32[]{:S(2)}) collective-permute-start(bf16[512,768]{1,0:T(8,128)(2,1)} %get-tuple-element.85.d_own), channel_id=1, source_target_pairs={{0,4},{1,5},{2,6},{3,7},{4,0},{5,1},{6,2},{7,3},{8,12},{9,13},{10,... | collective-permute-start | bytes 2359304 | tf_op jit(solution)/shard_map/ppermute | solution.py:602
  207.4 31.6 %all-to-all-start.3 = ((bf16[4,192,512]{2,1,0:T(8,128)(2,1)}), bf16[4,192,512]{2,1,0:T(8,128)(2,1)S(1)}, u32[]{:S(2)}, u32[]{:S(2)}) async-start(bf16[4,192,512]{2,1,0:T(8,128)(2,1)} %block.1), calls=%async_computation.3 | async-start | bytes 1572864 | tf_op jit(solution)/shard_map/all_to_all | solution.py:609
  244.1 3.7 collective-permute-start.20
  244.2 35.6 %all-to-all-start.4 = ((bf16[4,192,768]{2,1,0:T(8,128)(2,1)}), bf16[4,192,768]{2,1,0:T(8,128)(2,1)S(1)}, u32[]{:S(2)}, u32[]{:S(2)}) async-start(bf16[4,192,768]{2,1,0:T(8,128)(2,1)} %get-tuple-element.99), calls=%async_computation.5 | async-start | bytes 2359296 | tf_op jit(solution)/shard_map/all_to_all | solution.py:758
  247.8 34.3 %reduce-scatter.5.cloned.1.call-start = ((), (), s32[]{:S(2)}) async-start(), calls=%async_computation.9 | async-start | bytes 1474560 | tf_op jit(solution)/shard_map/reduce_scatter | solution.py:749
  250.1 88.6 %all-gather.9.cloned.1.call-start = ((), (), s32[]{:S(2)}) async-start(), calls=%async_computation.11 | async-start | bytes 2654208 | tf_op jit(solution)/shard_map/all_gather | solution.py:652
  286.2 2.7 collective-permute-start.21
  293.6 34.1 %all-to-all-start.5 = ((bf16[4,208,512]{2,1,0:T(8,128)(2,1)}), bf16[4,208,512]{2,1,0:T(8,128)(2,1)S(1)}, u32[]{:S(2)}, u32[]{:S(2)}) async-start(bf16[4,208,512]{2,1,0:T(8,128)(2,1)} %leave.1.rest_0_), calls=%async_computation.7 | async-start | bytes 1703936 | tf_op jit(solution)/shard_map/all_to_all | solution.py:609
  297.5 66.4 %all-gather.11.cloned.1.call-start = ((), (), s32[]{:S(2)}) async-start(), calls=%async_computation.12 | async-start | bytes 1327104 | tf_op jit(solution)/shard_map/all_gather | solution.py:652
  297.6 1.8 collective-permute-start.17
  299.5 12.3 %collective-permute-start.23 = (bf16[192,768]{1,0:T(8,128)(2,1)}, bf16[192,768]{1,0:T(8,128)(2,1)S(1)}, u32[]{:S(2)}, u32[]{:S(2)}) collective-permute-start(bf16[192,768]{1,0:T(8,128)(2,1)} %get-tuple-element.102), channel_id=1, source_target_pairs={{0,8},{1,9},{2,10},{3,11},{4,12},{5,13},{6,14},{7,15},{8,0},{9,1},... | collective-permute-start | bytes 884744 | tf_op jit(solution)/shard_map/ppermute | solution.py:602
  301.0 16.6 %collective-permute-start.24 = (bf16[192,768]{1,0:T(8,128)(2,1)}, bf16[192,768]{1,0:T(8,128)(2,1)S(1)}, u32[]{:S(2)}, u32[]{:S(2)}) collective-permute-start(bf16[192,768]{1,0:T(8,128)(2,1)} %get-tuple-element.103), channel_id=1, source_target_pairs={{0,16},{1,17},{2,18},{3,19},{4,20},{5,21},{6,22},{7,23},{8,24},{9,... | collective-permute-start | bytes 884744 | tf_op jit(solution)/shard_map/ppermute | solution.py:602
  302.5 19.9 %collective-permute-start.25 = (bf16[192,768]{1,0:T(8,128)(2,1)S(1)}, bf16[192,768]{1,0:T(8,128)(2,1)S(1)}, u32[]{:S(2)}, u32[]{:S(2)}) collective-permute-start(bf16[192,768]{1,0:T(8,128)(2,1)S(1)} %copy-done.60), channel_id=1, source_target_pairs={{0,24},{1,25},{2,26},{3,27},{4,28},{5,29},{6,30},{7,31},{8,16},{9,... | collective-permute-start | bytes 884744 | tf_op jit(solution)/shard_map/ppermute | solution.py:602
  304.5 27.2 %collective-permute-start.27 = (bf16[192,768]{1,0:T(8,128)(2,1)S(1)}, bf16[192,768]{1,0:T(8,128)(2,1)S(1)}, u32[]{:S(2)}, u32[]{:S(2)}) collective-permute-start(bf16[192,768]{1,0:T(8,128)(2,1)S(1)} %get-tuple-element.101.rest_0_.a), channel_id=1, source_target_pairs={{2,0},{3,1},{4,6},{5,7},{10,8},{11,9},{12,14},{13,15},{18,16},{19,... | collective-permute-start | bytes 884744 | tf_op jit(solution)/shard_map/ppermute | solution.py:602
  322.5 9.2 %collective-permute-start.26 = (bf16[192,768]{1,0:T(8,128)(2,1)S(1)}, bf16[192,768]{1,0:T(8,128)(2,1)S(1)}, u32[]{:S(2)}, u32[]{:S(2)}) collective-permute-start(bf16[192,768]{1,0:T(8,128)(2,1)S(1)} %sum_second.1), channel_id=1, source_target_pairs={{0,1},{1,0},{6,7},{7,6},{8,9},{9,8},{14,15},{15,14},{16,17},{17,16... | collective-permute-start | bytes 884744 | tf_op jit(solution)/shard_map/ppermute | solution.py:602
  326.4 10.5 %collective-permute-start.28 = (bf16[192,768]{1,0:T(8,128)(2,1)S(1)}, bf16[192,768]{1,0:T(8,128)(2,1)S(1)}, u32[]{:S(2)}, u32[]{:S(2)}) collective-permute-start(bf16[192,768]{1,0:T(8,128)(2,1)S(1)} %sum_second.1), channel_id=1, source_target_pairs={{2,1},{3,0},{4,7},{5,6},{10,9},{11,8},{12,15},{13,14},{18,17},{19,... | collective-permute-start | bytes 884744 | tf_op jit(solution)/shard_map/ppermute | solution.py:602
  327.9 9.4 %collective-permute-start.22 = (bf16[2,192,512]{2,1,0:T(8,128)(2,1)S(1)}, bf16[2,192,512]{2,1,0:T(8,128)(2,1)S(1)}, u32[]{:S(2)}, u32[]{:S(2)}) collective-permute-start(bf16[2,192,512]{2,1,0:T(8,128)(2,1)S(1)} %dynamic-slice_bitcast_fusion.1), channel_id=1, source_target_pairs={{0,4},{1,5},{2,6},{3,7},{4,0},{5,1},{6,2},{7,3},{8,12},{9,13},{10,... | collective-permute-start | bytes 1179656 | tf_op jit(solution)/shard_map/ppermute | solution.py:602
  337.1 1.6 collective-permute-start.29
  345.6 1.2 collective-permute-start.30
  346.8 3.6 collective-permute-start.31
  350.4 3.6 collective-permute-start.32
  (57 other events, 238.0 us)
Sparse Core Ops, SparseCore 0:
  28.5 49.1 all-gather.6
  187.8 55.1 reduce-scatter.2
  251.5 30.5 reduce-scatter.4
  286.3 37.8 all-gather.8
  341.8 22.0 all-gather.10
where the time goes:
time: 379 us; the launch traced here: 374 us
  Pallas kernels  144 us (38%)
  waiting for transfers between devices  82.8 us (22%)
  starting transfers between devices  60.9 us (16%)
  local copies, waits for them, and re-layouts  46.5 us (12%)
  between operations  20.5 us (5%)
  other arithmetic  18.5 us (5%)
    pallas_call x2, Pallas kernels, attn_bwd(): pl.pallas_call(partial(bwd_kernel, tq=tq, tk=tk, dh=dh, first=first), in_...  55.8 us
    ppermute x33, waiting for transfers between devices, move(): return lax.ppermute(v, ('row', 'head'), moves)  37.9 us
    pallas_call x2, Pallas kernels, attn_fwd(): pl.pallas_call(partial(fwd_kernel, tq=tq, tk=tk, dh=dh, part=part), in_sp...  37.4 us
    ppermute x33, starting transfers between devices, move(): return lax.ppermute(v, ('row', 'head'), moves)  34.9 us
    all_to_all x3, waiting for transfers between devices, deal_z(): return lax.all_to_all(v, 'head', 0, 0, tiled=True)  30.7 us
    unnamed x132, local copies, waits for them, and re-layouts  29.6 us
    pallas_call x12, Pallas kernels, call(): pl.pallas_call(kernel, in_specs=[pl.BlockSpec(memory_space=pltpu.SMEM)] *...  22.1 us
    pallas_call x2, Pallas kernels, mlp_first(): pl.pallas_call(partial(mlp_kernel, first=first), in_specs=[vmem] * (5 if...  17.6 us
  transfers between devices with their start and end apart: 44, of which 19 were waited for; matrix products, arithmetic and copies ran while one was open for 9% of the time, Pallas kernels for 34%

commit v1 on v0

--- a/solution.py
+++ b/solution.py
@@ -768,7 +768,7 @@
         leave_kernel, "leave", (near, move(away, 4), x_half, d_resid, gain1, vec2),
         (shape_of((heads_n, quarter + 16, half), bf16),), ahead=(first,),
     )
-    (second,) = sum_four(across(pieces), "sum_second", ahead=(send,))
+    (second,) = sum_four(across(pieces), "sum_second")
     got = deal_z(send)
     qkv_slice = give_z(first, second, got, mlp_grads)
     input_grad = collect(got[:, :quarter]).astype(f32)

time: 379 us -> 387 us (1.021)
  waiting for transfers between devices: 82.8 us -> 89 us
    ppermute x33, waiting for transfers between devices: 37.9 us -> 44.1 us  [move(): return lax.ppermute(v, ('row', 'head'), moves)]
    unnamed x132 -> x130, local copies, waits for them, and re-layouts: 29.6 us -> 29.6 us
  transfers between devices with their start and end apart: 44 -> 44, of which waited for: 19 -> 20; matrix products, arithmetic and copies ran while one was open for 9% -> 9% of each run, Pallas kernels for 34% -> 33%
where the time goes in v1:
time: 387 us; the launch traced here: 382 us
  Pallas kernels  144 us (37%)
  waiting for transfers between devices  89 us (23%)
  starting transfers between devices  61.8 us (16%)
  local copies, waits for them, and re-layouts  46.5 us (12%)
  between operations  20.4 us (5%)
  other arithmetic  19.4 us (5%)
    pallas_call x2, Pallas kernels, attn_bwd(): pl.pallas_call(partial(bwd_kernel, tq=tq, tk=tk, dh=dh, first=first), in_...  55.8 us
    ppermute x33, waiting for transfers between devices, move(): return lax.ppermute(v, ('row', 'head'), moves)  44.1 us
    pallas_call x2, Pallas kernels, attn_fwd(): pl.pallas_call(partial(fwd_kernel, tq=tq, tk=tk, dh=dh, part=part), in_sp...  37.4 us
    ppermute x33, starting transfers between devices, move(): return lax.ppermute(v, ('row', 'head'), moves)  35.8 us
    all_to_all x3, waiting for transfers between devices, deal_z(): return lax.all_to_all(v, 'head', 0, 0, tiled=True)  30.7 us
    unnamed x130, local copies, waits for them, and re-layouts  29.6 us
    pallas_call x12, Pallas kernels, call(): pl.pallas_call(kernel, in_specs=[pl.BlockSpec(memory_space=pltpu.SMEM)] *...  22.1 us
    pallas_call x2, Pallas kernels, mlp_first(): pl.pallas_call(partial(mlp_kernel, first=first), in_specs=[vmem] * (5 if...  17.6 us
  transfers between devices with their start and end apart: 44, of which 20 were waited for; matrix products, arithmetic and copies ran while one was open for 9% of the time, Pallas kernels for 33%

profile of v1, /device:TPU:0, one launch (start us, length us, event | category | flops | bytes accessed | tf_op | source)
XLA Modules:
  0.0 381.6 jit_solution(11643149463224569787)
XLA Ops:
  7.3 1.7 dynamic-slice_bitcast_fusion.7
  12.0 5.8 %collective-permute-start.1 = (bf16[208,768]{1,0:T(8,128)(2,1)}, bf16[208,768]{1,0:T(8,128)(2,1)S(1)}, u32[]{:S(2)}, u32[]{:S(2)}) collective-permute-start(bf16[208,768]{1,0:T(8,128)(2,1)} %pad_maximum_fusion.8), channel_id=1, source_target_pairs={{0,2},{1,3},{6,4},{7,5},{8,10},{9,11},{14,12},{15,13},{16,18},{17,... | collective-permute-start | bytes 958472 | tf_op jit(solution)/shard_map/ppermute | solution.py:602
  18.7 3.5 collective-permute-start.5
  28.4 3.7 collective-permute-done.5
  34.2 5.3 %all-to-all-start = ((bf16[4,192,512]{2,1,0:T(8,128)(2,1)}), bf16[4,192,512]{2,1,0:T(8,128)(2,1)S(1)}, u32[]{:S(2)}, u32[]{:S(2)}) async-start(bf16[4,192,512]{2,1,0:T(8,128)(2,1)} %pad_maximum_fusion.2), calls=%async_computation | async-start | bytes 1572864 | tf_op jit(solution)/shard_map/all_to_all | solution.py:609
  39.6 1.6 collective-permute-start.7
  41.1 1.5 collective-permute-start.8
  45.6 30.7 %all-to-all-done.dealt_ref = bf16[4,192,512]{2,1,0:T(8,128)(2,1)S(1)} async-done(((bf16[4,192,512]{2,1,0:T(8,128)(2,1)}), bf16[4,192,512]{2,1,0:T(8,128)(2,1)S(1)}, u32[]{:S(2)}, u32[]{:S(2)}) %all-to-all-start) | async-done | bytes 786464 | tf_op jit(solution)/shard_map/all_to_all | solution.py:609
  76.3 1.7 enter.1
  78.6 2.2 slice_bitcast_fusion
  80.8 1.6 broadcast_in_dim.19
  82.4 4.7 %all-to-all-start.1 = ((bf16[8,192,768]{2,1,0:T(8,128)(2,1)}), bf16[8,192,768]{2,1,0:T(8,128)(2,1)}, u32[]{:S(2)}, u32[]{:S(2)}) async-start(bf16[8,192,768]{2,1,0:T(8,128)(2,1)} %bitcast.168), calls=%async_computation.1 | async-start | bytes 4718592 | tf_op jit(solution)/shard_map/all_to_all | solution.py:687
  87.1 17.7 %attn_fwd.2 = (bf16[1024,192]{1,0:T(8,128)(2,1)S(1)}, f32[1024,8]{1,0:T(8,128)S(1)}, bf16[3,1024,256]{2,1,0:T(8,128)(2,1)}, bf16[3,1024,256]{2,1,0:T(8,128)(2,1)...) custom-call(s32[1]{0:T(128)} %bitcast.20.at_ref, ...), custom_call_target="tpu_custom_call" | custom-call | flops 27000000512 | bytes 10000000 | tf_op jit(solution)/shard_map/attn_fwd/pallas_call | solution.py:143
  107.9 2.3 fusion.7
  110.2 2.0 collective-permute-start.11
  112.2 2.4 collective-permute-start.12
  114.6 1.6 broadcast_in_dim.21
  116.2 19.7 %attn_fwd.3 = (bf16[1024,192]{1,0:T(8,128)(2,1)S(1)}, f32[1024,8]{1,0:T(8,128)S(1)}, f32[512,768]{1,0:T(8,128)}, bf16[512,768]{1,0:T(8,128)(2,1)}, bf16[3,1024,2...) custom-call(s32[1]{0:T(128)} %bitcast.20.at_ref, ...), custom_call_target="tpu_custom_call" | custom-call | flops 27000000512 | bytes 10000000 | tf_op jit(solution)/shard_map/attn_fwd/pallas_call | solution.py:143
  138.2 4.5 %all-to-all-start.2 = ((bf16[8,192,768]{2,1,0:T(8,128)(2,1)}), bf16[8,192,768]{2,1,0:T(8,128)(2,1)}, u32[]{:S(2)}, u32[]{:S(2)}) async-start(bf16[8,192,768]{2,1,0:T(8,128)(2,1)} %bitcast.171), calls=%async_computation.2 | async-start | bytes 4718592 | tf_op jit(solution)/shard_map/all_to_all | solution.py:687
  148.6 1.7 collective-permute-done.13.got_ref
  154.0 2.0 collective-permute-done.14.n_oth
  155.9 8.3 %mlp_first.2 = (bf16[1024,768]{1,0:T(8,128)(2,1)S(1)}, bf16[1024,768]{1,0:T(8,128)(2,1)}, f32[1024,768]{1,0:T(8,128)}) custom-call(bf16[512,768]{1,0:T(8,128)(2,1)S(1)} %get-tuple-element.69.n_own, bf16[512,768]{1,0:T(8,128)(2,1)S(1)} %collective-permute-done.14.n_oth, bf16[512,768]{1,0:T(8,128)(2,1)S(1)} %get-tuple-element.70.dy_own.dy_ref, ...), custom_call_target="tpu_custom_call" | custom-call | flops 2000000000 | bytes 2000000 | tf_op jit(solution)/shard_map/mlp_first/pallas_call | solution.py:368
  164.2 5.5 %mlp_second.2.rest_1_.rest_0_ = bf16[4,2,2,192,768]{4,3,2,1,0:T(8,128)(2,1)} custom-call(bf16[512,768]{1,0:T(8,128)(2,1)S(1)} %get-tuple-element.69.n_own, bf16[512,768]{1,0:T(8,128)(2,1)S(1)} %collective-permute-done.14.n_oth, bf16[512,768]{1,0:T(8,128)(2,1)S(1)} %get-tuple-element.70.dy_own.dy_ref, bf16[512,768]{1,0:T(8,128)(2,1)S(1)} %collective-permute-done.15.dy_oth, ...), custom_call_target="tpu_custom_call" | custom-call | flops 2000000000 | bytes 2000000 | tf_op jit(solution)/shard_map/mlp_second/pallas_call | solution.py:399
  172.2 9.4 %mlp_first.3 = (bf16[1024,768]{1,0:T(8,128)(2,1)S(1)}, bf16[1024,768]{1,0:T(8,128)(2,1)}, f32[512,768]{1,0:T(8,128)}, bf16[512,768]{1,0:T(8,128)(2,1)}) custom-call(bf16[512,768]{1,0:T(8,128)(2,1)S(1)} %get-tuple-element.69.n_own, bf16[512,768]{1,0:T(8,128)(2,1)S(1)} %collective-permute-done.14.n_oth, bf16[512,768]{1,0:T(8,128)(2,1)S(1)} %get-tuple-element.70.dy_own.dy_ref, ...), custom_call_target="tpu_custom_call" | custom-call | flops 2000000000 | bytes 2000000 | tf_op jit(solution)/shard_map/mlp_first/pallas_call | solution.py:368
  181.6 6.0 %mlp_second.3.rest_0_ = bf16[4,2,2,192,768]{4,3,2,1,0:T(8,128)(2,1)} custom-call(bf16[512,768]{1,0:T(8,128)(2,1)S(1)} %get-tuple-element.69.n_own, bf16[512,768]{1,0:T(8,128)(2,1)S(1)} %collective-permute-done.14.n_oth, bf16[512,768]{1,0:T(8,128)(2,1)S(1)} %get-tuple-element.70.dy_own.dy_ref, ...), custom_call_target="tpu_custom_call", output_to_operand_aliasing={{}: (6, {})} | custom-call | flops 2000000000 | bytes 2000000 | tf_op jit(solution)/shard_map/mlp_second/pallas_call | solution.py:399
  190.4 6.5 %mlp_out.1 = (f32[512,768]{1,0:T(8,128)S(1)}, bf16[512,768]{1,0:T(8,128)(2,1)}) custom-call(bf16[1024,768]{1,0:T(8,128)(2,1)S(1)} %copy-done.5, bf16[1024,768]{1,0:T(8,128)(2,1)S(1)} %copy-done.7, bf16[8,192,768]{2,1,0:T(8,128)(2,1)} %all-to-all-done.1.rest_2_.w_ref.w_a, bf16[8,192,768]{2,1,0:T(8,128)(2,1)} %all-to-all-done.2.w_ref.w_b, ...), custom_call_target="tpu_custom_call" | custom-call | flops 1000000000 | bytes 4000000 | tf_op jit(solution)/shard_map/mlp_out/pallas_call | solution.py:426
  198.1 3.9 %middle_back.1 = (f32[512,768]{1,0:T(8,128)S(1)}, bf16[512,768]{1,0:T(8,128)(2,1)}, f32[2,768]{1,0:T(2,128)S(1)}) custom-call(f32[512,768]{1,0:T(8,128)S(1)} %copy-done.18, bf16[512,768]{1,0:T(8,128)(2,1)S(1)} %collective-permute-done.18.got_ref, f32[512,768]{1,0:T(8,128)} %copy-done.2, bf16[512,768]{1,0:T(8,128)(2,1)S(1)} %get-tuple-element.70.dy_own.dy_ref, ...), custom_call_target="tpu_custom_call" | custom-call | flops 1000000000 | bytes 4000000 | tf_op jit(solution)/shard_map/middle_back/pallas_call | solution.py:426
  207.3 3.7 all-to-all-start.3
  211.9 26.4 %attn_bwd.2 = (bf16[4,192,768]{2,1,0:T(8,128)(2,1)}, bf16[1024,576]{1,0:T(8,128)(2,1)}, s32[1]{0:T(128)}) custom-call(s32[1]{0:T(128)} %bitcast.20.at_ref, s32[1,1024]{1,0:T(1,128)} %bitcast.160, bf16[1024,576]{1,0:T(8,128)(2,1)} %get-tuple-element.88.qkv_ref, s32[1024,1]{1,0:T(8,128)} %copy.43.segc_ref, s32[1,1024]{1,0:T(1,128)} %bitcast.161, ...), custom_call_target="tpu_custom_call" | custom-call | flops 41999998976 | bytes 20000000 | tf_op jit(solution)/shard_map/attn_bwd/pallas_call | solution.py:294
  240.8 2.2 reduce-scatter.3.cloned.1.call-done
  244.2 3.5 all-to-all-start.4
  250.3 29.4 %attn_bwd.3 = (bf16[192,768]{1,0:T(8,128)(2,1)}, bf16[192,768]{1,0:T(8,128)(2,1)}, bf16[192,768]{1,0:T(8,128)(2,1)}, bf16[192,768]{1,0:T(8,128)(2,1)}, f32[512,7...) custom-call(s32[1]{0:T(128)} %bitcast.20.at_ref, s32[1,1024]{1,0:T(1,128)} %bitcast.162, ...), custom_call_target="tpu_custom_call" | custom-call | flops 41999998976 | bytes 20000000 | tf_op jit(solution)/shard_map/attn_bwd/pallas_call | solution.py:294
  286.2 2.6 collective-permute-done.21.got_ref
  290.0 3.6 leave.1
  293.6 3.9 %all-to-all-start.5 = ((bf16[4,208,512]{2,1,0:T(8,128)(2,1)}), bf16[4,208,512]{2,1,0:T(8,128)(2,1)S(1)}, u32[]{:S(2)}, u32[]{:S(2)}) async-start(bf16[4,208,512]{2,1,0:T(8,128)(2,1)} %leave.1), calls=%async_computation.7 | async-start | bytes 1703936 | tf_op jit(solution)/shard_map/all_to_all | solution.py:609
  297.8 1.6 collective-permute-done.17
  300.5 1.5 collective-permute-start.23
  305.6 8.4 %collective-permute-done.23.b = bf16[192,768]{1,0:T(8,128)(2,1)S(1)} collective-permute-done((bf16[192,768]{1,0:T(8,128)(2,1)}, bf16[192,768]{1,0:T(8,128)(2,1)S(1)}, u32[]{:S(2)}, u32[]{:S(2)}) %collective-permute-start.23) | collective-permute-done | bytes 294944 | tf_op jit(solution)/shard_map/ppermute | solution.py:602
  313.9 8.0 %collective-permute-done.24.c = bf16[192,768]{1,0:T(8,128)(2,1)S(1)} collective-permute-done((bf16[192,768]{1,0:T(8,128)(2,1)}, bf16[192,768]{1,0:T(8,128)(2,1)S(1)}, u32[]{:S(2)}, u32[]{:S(2)}) %collective-permute-start.24) | collective-permute-done | bytes 294944 | tf_op jit(solution)/shard_map/ppermute | solution.py:602
  323.6 3.9 %collective-permute-start.26 = (bf16[192,768]{1,0:T(8,128)(2,1)S(1)}, bf16[192,768]{1,0:T(8,128)(2,1)S(1)}, u32[]{:S(2)}, u32[]{:S(2)}) collective-permute-start(bf16[192,768]{1,0:T(8,128)(2,1)S(1)} %sum_second.1), channel_id=1, source_target_pairs={{0,1},{1,0},{6,7},{7,6},{8,9},{9,8},{14,15},{15,14},{16,17},{17,16... | collective-permute-start | bytes 884744 | tf_op jit(solution)/shard_map/ppermute | solution.py:602
  330.2 1.8 collective-permute-start.22
  332.0 2.1 maximum_bitcast_fusion
  334.1 3.9 %collective-permute-done.28.d = bf16[192,768]{1,0:T(8,128)(2,1)S(1)} collective-permute-done((bf16[192,768]{1,0:T(8,128)(2,1)S(1)}, bf16[192,768]{1,0:T(8,128)(2,1)S(1)}, u32[]{:S(2)}, u32[]{:S(2)}) %collective-permute-start.28) | collective-permute-done | bytes 294944 | tf_op jit(solution)/shard_map/ppermute | solution.py:602
  338.0 7.1 %collective-permute-done.27.c = bf16[192,768]{1,0:T(8,128)(2,1)S(1)} collective-permute-done((bf16[192,768]{1,0:T(8,128)(2,1)S(1)}, bf16[192,768]{1,0:T(8,128)(2,1)S(1)}, u32[]{:S(2)}, u32[]{:S(2)}) %collective-permute-start.27) | collective-permute-done | bytes 294944 | tf_op jit(solution)/shard_map/ppermute | solution.py:602
  346.9 1.7 copy-done.8
  356.3 1.7 bitcast_convert_fusion.1
  360.0 1.7 bitcast_convert_fusion
  362.7 9.3 %all-gather.11.cloned.1.call-done = bf16[768,768]{1,0:T(8,128)(2,1)} async-done(((bf16[96,768]{1,0:T(8,128)(2,1)}), bf16[768,768]{1,0:T(8,128)(2,1)}) %all-gather.11.cloned.1.call-update) | async-done | bytes 1179664 | tf_op jit(solution)/shard_map/all_gather | solution.py:652
  (278 shorter events, 76.3 us)
Async XLA Ops:
  7.2 71.4 %all-gather.7.cloned.1.call-start = ((), (), s32[]{:S(2)}) async-start(), calls=%async_computation.10 | async-start | bytes 1474560 | tf_op jit(solution)/shard_map/all_gather | solution.py:685
  9.0 23.1 %collective-permute-start.2 = (bf16[2,192,512]{2,1,0:T(8,128)(2,1)S(1)}, bf16[2,192,512]{2,1,0:T(8,128)(2,1)}, u32[]{:S(2)}, u32[]{:S(2)}) collective-permute-start(bf16[2,192,512]{2,1,0:T(8,128)(2,1)S(1)} %pad_maximum_fusion.5), channel_id=1, source_target_pairs={{0,4},{1,5},{2,6},{3,7},{4,0},{5,1},{6,2},{7,3},{8,12},{9,13},{10,... | collective-permute-start | bytes 1179656 | tf_op jit(solution)/shard_map/ppermute | solution.py:602
  9.9 1.2 collective-permute-start
  12.0 12.7 %collective-permute-start.1 = (bf16[208,768]{1,0:T(8,128)(2,1)}, bf16[208,768]{1,0:T(8,128)(2,1)S(1)}, u32[]{:S(2)}, u32[]{:S(2)}) collective-permute-start(bf16[208,768]{1,0:T(8,128)(2,1)} %pad_maximum_fusion.8), channel_id=1, source_target_pairs={{0,2},{1,3},{6,4},{7,5},{8,10},{9,11},{14,12},{15,13},{16,18},{17,... | collective-permute-start | bytes 958472 | tf_op jit(solution)/shard_map/ppermute | solution.py:602
  18.6 25.2 %collective-permute-start.3 = (bf16[2,192,512]{2,1,0:T(8,128)(2,1)}, bf16[2,192,512]{2,1,0:T(8,128)(2,1)}, u32[]{:S(2)}, u32[]{:S(2)}) collective-permute-start(bf16[2,192,512]{2,1,0:T(8,128)(2,1)} %pad_maximum_fusion.7), channel_id=1, source_target_pairs={{0,4},{1,5},{2,6},{3,7},{4,0},{5,1},{6,2},{7,3},{8,12},{9,13},{10,... | collective-permute-start | bytes 1179656 | tf_op jit(solution)/shard_map/ppermute | solution.py:602
  18.6 57.7 %copy-start.34 = (f32[1,768]{1,0:T(1,128)}, f32[1,768]{1,0:T(1,128)S(1)}, u32[]{:S(2)}) copy-start(f32[1,768]{1,0:T(1,128)S(1)} %reshape.171.gain_ref) | copy-start | bytes 9220
  18.7 13.4 %collective-permute-start.5 = (bf16[208,768]{1,0:T(8,128)(2,1)}, bf16[208,768]{1,0:T(8,128)(2,1)S(1)}, u32[]{:S(2)}, u32[]{:S(2)}) collective-permute-start(bf16[208,768]{1,0:T(8,128)(2,1)} %pad_maximum_fusion.8), channel_id=1, source_target_pairs={{0,1},{1,0},{6,7},{7,6},{8,9},{9,8},{14,15},{15,14},{16,17},{17,16... | collective-permute-start | bytes 958472 | tf_op jit(solution)/shard_map/ppermute | solution.py:602
  22.2 9.9 %collective-permute-start.6 = (bf16[208,768]{1,0:T(8,128)(2,1)}, bf16[208,768]{1,0:T(8,128)(2,1)S(1)}, u32[]{:S(2)}, u32[]{:S(2)}) collective-permute-start(bf16[208,768]{1,0:T(8,128)(2,1)} %pad_maximum_fusion.8), channel_id=1, source_target_pairs={{0,3},{1,2},{6,5},{7,4},{8,11},{9,10},{14,13},{15,12},{16,19},{17,... | collective-permute-start | bytes 958472 | tf_op jit(solution)/shard_map/ppermute | solution.py:602
  23.7 92.5 %copy-start.33 = (s32[1024]{0:T(1024)}, s32[1024]{0:T(1024)S(1)}, u32[]{:S(2)}) copy-start(s32[1024]{0:T(1024)S(1)} %fusion.20) | copy-start | bytes 12292
  34.2 42.1 %all-to-all-start = ((bf16[4,192,512]{2,1,0:T(8,128)(2,1)}), bf16[4,192,512]{2,1,0:T(8,128)(2,1)S(1)}, u32[]{:S(2)}, u32[]{:S(2)}) async-start(bf16[4,192,512]{2,1,0:T(8,128)(2,1)} %pad_maximum_fusion.2), calls=%async_computation | async-start | bytes 1572864 | tf_op jit(solution)/shard_map/all_to_all | solution.py:609
  39.6 47.5 %collective-permute-start.7 = (bf16[2,192,768]{2,1,0:T(8,128)(2,1)S(1)}, bf16[2,192,768]{2,1,0:T(8,128)(2,1)}, u32[]{:S(2)}, u32[]{:S(2)}) collective-permute-start(bf16[2,192,768]{2,1,0:T(8,128)(2,1)S(1)} %pad_maximum_fusion.3.rest_0_), channel_id=1, source_target_pairs={{0,8},{1,9},{2,10},{3,11},{4,12},{5,13},{6,14},{7,15},{8,0},{9,1},... | collective-permute-start | bytes 1769480 | tf_op jit(solution)/shard_map/ppermute | solution.py:602
  41.1 45.9 %collective-permute-start.8 = (bf16[2,192,768]{2,1,0:T(8,128)(2,1)S(1)}, bf16[2,192,768]{2,1,0:T(8,128)(2,1)}, u32[]{:S(2)}, u32[]{:S(2)}) collective-permute-start(bf16[2,192,768]{2,1,0:T(8,128)(2,1)S(1)} %pad_maximum_fusion.3.rest_0_), channel_id=1, source_target_pairs={{0,16},{1,17},{2,18},{3,19},{4,20},{5,21},{6,22},{7,23},{8,24},{9,... | collective-permute-start | bytes 1769480 | tf_op jit(solution)/shard_map/ppermute | solution.py:602
  42.6 44.4 %collective-permute-start.9 = (bf16[2,192,768]{2,1,0:T(8,128)(2,1)S(1)}, bf16[2,192,768]{2,1,0:T(8,128)(2,1)}, u32[]{:S(2)}, u32[]{:S(2)}) collective-permute-start(bf16[2,192,768]{2,1,0:T(8,128)(2,1)S(1)} %pad_maximum_fusion.3.rest_0_), channel_id=1, source_target_pairs={{0,24},{1,25},{2,26},{3,27},{4,28},{5,29},{6,30},{7,31},{8,16},{9,... | collective-permute-start | bytes 1769480 | tf_op jit(solution)/shard_map/ppermute | solution.py:602
  78.0 72.3 %copy-start.21 = (bf16[512,768]{1,0:T(8,128)(2,1)}, bf16[512,768]{1,0:T(8,128)(2,1)S(1)}, u32[]{:S(2)}) copy-start(bf16[512,768]{1,0:T(8,128)(2,1)S(1)} %get-tuple-element.59.x_ref) | copy-start | bytes 2359300
  78.0 9.0 %collective-permute-start.4 = (bf16[512,768]{1,0:T(8,128)(2,1)}, bf16[512,768]{1,0:T(8,128)(2,1)S(1)}, u32[]{:S(2)}, u32[]{:S(2)}) collective-permute-start(bf16[512,768]{1,0:T(8,128)(2,1)} %get-tuple-element.60.own_ref.rest_0_), channel_id=1, source_target_pairs={{0,4},{1,5},{2,6},{3,7},{4,0},{5,1},{6,2},{7,3},{8,12},{9,13},{10,... | collective-permute-start | bytes 2359304 | tf_op jit(solution)/shard_map/ppermute | solution.py:602
  78.6 37.6 %copy-start.29 = (f32[3,16,1024]{2,1,0:T(8,128)}, f32[3,16,1024]{2,1,0:T(8,128)S(1)}, u32[]{:S(2)}) copy-start(f32[3,16,1024]{2,1,0:T(8,128)S(1)} %fusion.9.hit_ref) | copy-start | bytes 589828
  82.4 55.9 %all-to-all-start.1 = ((bf16[8,192,768]{2,1,0:T(8,128)(2,1)}), bf16[8,192,768]{2,1,0:T(8,128)(2,1)}, u32[]{:S(2)}, u32[]{:S(2)}) async-start(bf16[8,192,768]{2,1,0:T(8,128)(2,1)} %bitcast.168), calls=%async_computation.1 | async-start | bytes 4718592 | tf_op jit(solution)/shard_map/all_to_all | solution.py:687
  110.2 32.6 %collective-permute-start.10 = (bf16[192,512]{1,0:T(8,128)(2,1)}, bf16[192,512]{1,0:T(8,128)(2,1)S(1)}, u32[]{:S(2)}, u32[]{:S(2)}) collective-permute-start(bf16[192,512]{1,0:T(8,128)(2,1)} %get-tuple-element.122.rest_9_), channel_id=1, source_target_pairs={{0,1},{1,0},{2,3},{3,2},{4,5},{5,4},{6,7},{7,6},{8,9},{9,8},{10,11... | collective-permute-start | bytes 589832 | tf_op jit(solution)/shard_map/ppermute | solution.py:602
  110.2 32.6 %collective-permute-start.11 = (bf16[192,512]{1,0:T(8,128)(2,1)}, bf16[192,512]{1,0:T(8,128)(2,1)S(1)}, u32[]{:S(2)}, u32[]{:S(2)}) collective-permute-start(bf16[192,512]{1,0:T(8,128)(2,1)} %get-tuple-element.123.rest_10_), channel_id=1, source_target_pairs={{0,2},{1,3},{2,0},{3,1},{4,6},{5,7},{6,4},{7,5},{8,10},{9,11},{10,... | collective-permute-start | bytes 589832 | tf_op jit(solution)/shard_map/ppermute | solution.py:602
  112.2 31.3 %collective-permute-start.12 = (bf16[192,512]{1,0:T(8,128)(2,1)}, bf16[192,512]{1,0:T(8,128)(2,1)}, u32[]{:S(2)}, u32[]{:S(2)}) collective-permute-start(bf16[192,512]{1,0:T(8,128)(2,1)} %get-tuple-element.120.rest_11_), channel_id=1, source_target_pairs={{0,3},{1,2},{2,1},{3,0},{4,7},{5,6},{6,5},{7,4},{8,11},{9,10},{10,... | collective-permute-start | bytes 589832 | tf_op jit(solution)/shard_map/ppermute | solution.py:602
  138.2 34.0 %all-to-all-start.2 = ((bf16[8,192,768]{2,1,0:T(8,128)(2,1)}), bf16[8,192,768]{2,1,0:T(8,128)(2,1)}, u32[]{:S(2)}, u32[]{:S(2)}) async-start(bf16[8,192,768]{2,1,0:T(8,128)(2,1)} %bitcast.171), calls=%async_computation.2 | async-start | bytes 4718592 | tf_op jit(solution)/shard_map/all_to_all | solution.py:687
  142.7 100.2 %reduce-scatter.3.cloned.1.call-start = ((), (), s32[]{:S(2)}) async-start(), calls=%async_computation.8 | async-start | bytes 5898240 | tf_op jit(solution)/shard_map/reduce_scatter | solution.py:734
  148.0 2.3 collective-permute-start.13
  148.3 5.6 %collective-permute-start.15 = (bf16[512,768]{1,0:T(8,128)(2,1)S(1)}, bf16[512,768]{1,0:T(8,128)(2,1)S(1)}, u32[]{:S(2)}, u32[]{:S(2)}) collective-permute-start(bf16[512,768]{1,0:T(8,128)(2,1)S(1)} %get-tuple-element.70.dy_own.dy_ref), channel_id=1, source_target_pairs={{0,4},{1,5},{2,6},{3,7},{4,0},{5,1},{6,2},{7,3},{8,12},{9,13},{10,... | collective-permute-start | bytes 2359304 | tf_op jit(solution)/shard_map/ppermute | solution.py:602
  153.6 2.3 collective-permute-start.14
  187.6 10.4 %collective-permute-start.18 = (bf16[512,768]{1,0:T(8,128)(2,1)}, bf16[512,768]{1,0:T(8,128)(2,1)S(1)}, u32[]{:S(2)}, u32[]{:S(2)}) collective-permute-start(bf16[512,768]{1,0:T(8,128)(2,1)} %get-tuple-element.84), channel_id=1, source_target_pairs={{0,4},{1,5},{2,6},{3,7},{4,0},{5,1},{6,2},{7,3},{8,12},{9,13},{10,... | collective-permute-start | bytes 2359304 | tf_op jit(solution)/shard_map/ppermute | solution.py:602
  198.1 6.5 %collective-permute-start.16 = (bf16[512,768]{1,0:T(8,128)(2,1)}, bf16[512,768]{1,0:T(8,128)(2,1)S(1)}, u32[]{:S(2)}, u32[]{:S(2)}) collective-permute-start(bf16[512,768]{1,0:T(8,128)(2,1)} %get-tuple-element.77.rest_3_), channel_id=1, source_target_pairs={{0,4},{1,5},{2,6},{3,7},{4,0},{5,1},{6,2},{7,3},{8,12},{9,13},{10,... | collective-permute-start | bytes 2359304 | tf_op jit(solution)/shard_map/ppermute | solution.py:602
  203.1 7.8 %collective-permute-start.19 = (bf16[512,768]{1,0:T(8,128)(2,1)}, bf16[512,768]{1,0:T(8,128)(2,1)S(1)}, u32[]{:S(2)}, u32[]{:S(2)}) collective-permute-start(bf16[512,768]{1,0:T(8,128)(2,1)} %get-tuple-element.85.d_own), channel_id=1, source_target_pairs={{0,4},{1,5},{2,6},{3,7},{4,0},{5,1},{6,2},{7,3},{8,12},{9,13},{10,... | collective-permute-start | bytes 2359304 | tf_op jit(solution)/shard_map/ppermute | solution.py:602
  207.3 31.6 %all-to-all-start.3 = ((bf16[4,192,512]{2,1,0:T(8,128)(2,1)}), bf16[4,192,512]{2,1,0:T(8,128)(2,1)S(1)}, u32[]{:S(2)}, u32[]{:S(2)}) async-start(bf16[4,192,512]{2,1,0:T(8,128)(2,1)} %block.1), calls=%async_computation.3 | async-start | bytes 1572864 | tf_op jit(solution)/shard_map/all_to_all | solution.py:609
  244.1 3.7 collective-permute-start.20
  244.2 35.6 %all-to-all-start.4 = ((bf16[4,192,768]{2,1,0:T(8,128)(2,1)}), bf16[4,192,768]{2,1,0:T(8,128)(2,1)S(1)}, u32[]{:S(2)}, u32[]{:S(2)}) async-start(bf16[4,192,768]{2,1,0:T(8,128)(2,1)} %get-tuple-element.99), calls=%async_computation.5 | async-start | bytes 2359296 | tf_op jit(solution)/shard_map/all_to_all | solution.py:758
  247.7 34.3 %reduce-scatter.5.cloned.1.call-start = ((), (), s32[]{:S(2)}) async-start(), calls=%async_computation.9 | async-start | bytes 1474560 | tf_op jit(solution)/shard_map/reduce_scatter | solution.py:749
  250.1 96.8 %all-gather.9.cloned.1.call-start = ((), (), s32[]{:S(2)}) async-start(), calls=%async_computation.11 | async-start | bytes 2654208 | tf_op jit(solution)/shard_map/all_gather | solution.py:652
  286.2 2.7 collective-permute-start.21
  293.6 36.5 %all-to-all-start.5 = ((bf16[4,208,512]{2,1,0:T(8,128)(2,1)}), bf16[4,208,512]{2,1,0:T(8,128)(2,1)S(1)}, u32[]{:S(2)}, u32[]{:S(2)}) async-start(bf16[4,208,512]{2,1,0:T(8,128)(2,1)} %leave.1), calls=%async_computation.7 | async-start | bytes 1703936 | tf_op jit(solution)/shard_map/all_to_all | solution.py:609
  297.5 74.5 %all-gather.11.cloned.1.call-start = ((), (), s32[]{:S(2)}) async-start(), calls=%async_computation.12 | async-start | bytes 1327104 | tf_op jit(solution)/shard_map/all_gather | solution.py:652
  297.6 1.9 collective-permute-start.17
  300.5 13.4 %collective-permute-start.23 = (bf16[192,768]{1,0:T(8,128)(2,1)}, bf16[192,768]{1,0:T(8,128)(2,1)S(1)}, u32[]{:S(2)}, u32[]{:S(2)}) collective-permute-start(bf16[192,768]{1,0:T(8,128)(2,1)} %get-tuple-element.102), channel_id=1, source_target_pairs={{0,8},{1,9},{2,10},{3,11},{4,12},{5,13},{6,14},{7,15},{8,0},{9,1},... | collective-permute-start | bytes 884744 | tf_op jit(solution)/shard_map/ppermute | solution.py:602
  302.1 19.9 %collective-permute-start.24 = (bf16[192,768]{1,0:T(8,128)(2,1)}, bf16[192,768]{1,0:T(8,128)(2,1)S(1)}, u32[]{:S(2)}, u32[]{:S(2)}) collective-permute-start(bf16[192,768]{1,0:T(8,128)(2,1)} %get-tuple-element.103), channel_id=1, source_target_pairs={{0,16},{1,17},{2,18},{3,19},{4,20},{5,21},{6,22},{7,23},{8,24},{9,... | collective-permute-start | bytes 884744 | tf_op jit(solution)/shard_map/ppermute | solution.py:602
  303.5 19.9 %collective-permute-start.25 = (bf16[192,768]{1,0:T(8,128)(2,1)}, bf16[192,768]{1,0:T(8,128)(2,1)S(1)}, u32[]{:S(2)}, u32[]{:S(2)}) collective-permute-start(bf16[192,768]{1,0:T(8,128)(2,1)} %get-tuple-element.104), channel_id=1, source_target_pairs={{0,24},{1,25},{2,26},{3,27},{4,28},{5,29},{6,30},{7,31},{8,16},{9,... | collective-permute-start | bytes 884744 | tf_op jit(solution)/shard_map/ppermute | solution.py:602
  323.6 10.5 %collective-permute-start.26 = (bf16[192,768]{1,0:T(8,128)(2,1)S(1)}, bf16[192,768]{1,0:T(8,128)(2,1)S(1)}, u32[]{:S(2)}, u32[]{:S(2)}) collective-permute-start(bf16[192,768]{1,0:T(8,128)(2,1)S(1)} %sum_second.1), channel_id=1, source_target_pairs={{0,1},{1,0},{6,7},{7,6},{8,9},{9,8},{14,15},{15,14},{16,17},{17,16... | collective-permute-start | bytes 884744 | tf_op jit(solution)/shard_map/ppermute | solution.py:602
  327.5 10.5 %collective-permute-start.28 = (bf16[192,768]{1,0:T(8,128)(2,1)S(1)}, bf16[192,768]{1,0:T(8,128)(2,1)S(1)}, u32[]{:S(2)}, u32[]{:S(2)}) collective-permute-start(bf16[192,768]{1,0:T(8,128)(2,1)S(1)} %sum_second.1), channel_id=1, source_target_pairs={{2,1},{3,0},{4,7},{5,6},{10,9},{11,8},{12,15},{13,14},{18,17},{19,... | collective-permute-start | bytes 884744 | tf_op jit(solution)/shard_map/ppermute | solution.py:602
  328.8 16.3 %collective-permute-start.27 = (bf16[192,768]{1,0:T(8,128)(2,1)S(1)}, bf16[192,768]{1,0:T(8,128)(2,1)S(1)}, u32[]{:S(2)}, u32[]{:S(2)}) collective-permute-start(bf16[192,768]{1,0:T(8,128)(2,1)S(1)} %get-tuple-element.101.rest_0_.a), channel_id=1, source_target_pairs={{2,0},{3,1},{4,6},{5,7},{10,8},{11,9},{12,14},{13,15},{18,16},{19,... | collective-permute-start | bytes 884744 | tf_op jit(solution)/shard_map/ppermute | solution.py:602
  330.2 15.1 %collective-permute-start.22 = (bf16[2,192,512]{2,1,0:T(8,128)(2,1)S(1)}, bf16[2,192,512]{2,1,0:T(8,128)(2,1)S(1)}, u32[]{:S(2)}, u32[]{:S(2)}) collective-permute-start(bf16[2,192,512]{2,1,0:T(8,128)(2,1)S(1)} %dynamic-slice_bitcast_fusion.1), channel_id=1, source_target_pairs={{0,4},{1,5},{2,6},{3,7},{4,0},{5,1},{6,2},{7,3},{8,12},{9,13},{10,... | collective-permute-start | bytes 1179656 | tf_op jit(solution)/shard_map/ppermute | solution.py:602
  345.2 1.6 collective-permute-start.29
  353.7 1.2 collective-permute-start.30
  354.9 3.6 collective-permute-start.31
  358.5 3.6 collective-permute-start.32
  (56 other events, 234.1 us)
Sparse Core Ops, SparseCore 0:
  28.5 49.1 all-gather.6
  187.7 55.1 reduce-scatter.2
  251.4 30.5 reduce-scatter.4
  286.3 38.9 all-gather.8
  349.9 22.0 all-gather.10
